TPU v7x, 32 devices: a whole 2x2x4 slice. The times are simulated.
32 devices in a mesh: box: 8 (over z, x), grp: 4 (over y, core).
Axes of the slice: x: 2, y: 2, z: 4, core: 2. Of those that a mesh axis runs over, the one named last changes fastest.
Arguments:
- old_fields: float32 [3, 4, 32, 32, 1024], P(None, 'grp', 'box'), may hold values from -6 to 6, as said below
- old_count: int32 [4, 8], P('grp'), may hold values from 0 to 4, as said below
- neighbours: int32 [4, 16, 6], P('grp', 'box'), may hold values from -1 to 15, as said below
- parents: int32 [4, 16, 3], P('grp', 'box'), may hold values from 0 to 7, as said below
- coarse_source: float32 [4, 16, 8, 16, 256], P('grp', 'box'), may hold values from -6 to 6
Outputs:
- smoothed: float32 [4, 16, 32, 1024], P('grp', 'box')
- residual: float32 [4, 16, 32, 1024], P('grp', 'box')
- coarse_rhs: float32 [4, 16, 8, 16, 256], P('grp', 'box')
Inputs may be any that keep to these rules, and one draw needn't show every extreme that they name: `old_fields`: components 0, 1, 2 are the solution, the right side and the cell coefficient; the coefficient lies in [0.25, 4]. `old_count`: in each owner group the counts sum to 16, and the sum of the first j counts differs from j * 2 by at most 1 for every j; some device holds 4 boxes and some none. Neighbourhood is symmetric; the x- neighbour of a box lies in the previous run of 2 boxes along the curve, the x+ neighbour in the next run, the y and z neighbours in the box's own run. `parents`: the named coarse box belongs to the owner on the same curve position as the fine box; no two fine boxes name the same octant of the same coarse box.
All inputs are finite; a program needn't handle non-finite values.
Results may differ from a plain program's by a relative error of at most 0.0001.
Values sent between devices are 32-bit elements; how exact they have to be, the bound alone decides.
A program may use at most 64 MiB of HBM per device.

v0:
```python
import jax
import jax.numpy as jnp
from jax import lax
from jax.sharding import PartitionSpec as P

MASS_TERM = 0.25


def with_halo(cells, sides, width):
    for axis, dim in sides:
        count = lax.axis_size(axis)
        ends = count - 1
        head = lax.slice_in_dim(cells, 0, width, axis=dim)
        tail = lax.slice_in_dim(cells, cells.shape[dim] - width, cells.shape[dim], axis=dim)
        cells = jnp.concatenate(
            [
                lax.ppermute(tail, axis, [(i, (i + 1) % count) for i in range(ends)]),
                cells,
                lax.ppermute(head, axis, [((i + 1) % count, i) for i in range(ends)]),
            ],
            axis=dim,
        )
    return cells


def box_planes(box_field, box_edge):
    plane_cells = box_edge * box_edge
    return (
        box_field[:, 0, :],
        box_field[:, -1, :],
        box_field[:, :, :box_edge],
        box_field[:, :, plane_cells - box_edge :],
        box_field[:, :, 0::box_edge],
        box_field[:, :, box_edge - 1 :: box_edge],
    )


def ghost_planes(
    box_field,
    lower_table,
    upper_table,
    lower_offset,
    upper_offset,
    link_rows,
    first_box,
    keep_own,
    box_edge,
):
    planes = box_planes(box_field, box_edge)
    tables = (lower_table, upper_table, planes[3], planes[2], planes[5], planes[4])
    offsets = (lower_offset, upper_offset, first_box, first_box, first_box, first_box)
    results = []
    for face_id in range(6):
        fallback = planes[face_id] if keep_own else jnp.zeros_like(planes[face_id])
        target = link_rows[:, face_id]
        local_row = jnp.clip(target - offsets[face_id], 0, tables[face_id].shape[0] - 1)
        chosen = jnp.take(tables[face_id], local_row, axis=0)
        is_valid = (target >= 0).reshape((-1,) + (1,) * (chosen.ndim - 1))
        results.append(jnp.where(is_valid, chosen, fallback))
    return results


def beside_cells(box_field, planes, box_edge, low_mask, high_mask):
    plane_cells = box_field.shape[2]
    zero_column = jnp.zeros(box_field.shape[:2] + (1,), box_field.dtype)
    low_shift = jnp.concatenate([zero_column, box_field[:, :, :-1]], axis=2)
    high_shift = jnp.concatenate([box_field[:, :, 1:], zero_column], axis=2)
    return (
        jnp.concatenate([planes[0][:, None, :], box_field[:, :-1, :]], axis=1),
        jnp.concatenate([box_field[:, 1:, :], planes[1][:, None, :]], axis=1),
        jnp.concatenate([planes[2], box_field[:, :, : plane_cells - box_edge]], axis=2),
        jnp.concatenate([box_field[:, :, box_edge:], planes[3]], axis=2),
        jnp.where(low_mask, jnp.repeat(planes[4], box_edge, axis=2), low_shift),
        jnp.where(high_mask, jnp.repeat(planes[5], box_edge, axis=2), high_shift),
    )


def weighted_sum(weights, nearby):
    running = weights[0] * nearby[0]
    for face_id in range(1, 6):
        running = running + weights[face_id] * nearby[face_id]
    return running


def make_weights(coefficient, coef_ghosts, box_edge, low_mask, high_mask):
    weights = [
        0.5 * (coefficient + nearby_coef)
        for nearby_coef in beside_cells(coefficient, coef_ghosts, box_edge, low_mask, high_mask)
    ]
    diagonal = MASS_TERM + weights[0]
    for face_id in range(1, 6):
        diagonal = diagonal + weights[face_id]
    return (weights, diagonal)


def half_sweep(
    field, ghosts, right_side, weights, diagonal, parity_rows, colour, box_edge, low_mask, high_mask
):
    nearby = beside_cells(field, ghosts, box_edge, low_mask, high_mask)
    updated = (right_side + weighted_sum(weights, nearby)) / diagonal
    return jnp.where(parity_rows == colour, updated, field)


def fresh_faces(solution, box_count, box_edge):
    outgoing = jnp.concatenate([solution[:, 0], solution[:, box_edge - 1]], axis=0)
    arrived = with_halo(outgoing, (("box", 0),), box_count)
    return (arrived[:box_count], arrived[3 * box_count :])


def per_device(old_fields, old_count, neighbours, parents, coarse_source):
    box_edge = old_fields.shape[3]
    plane_cells = box_edge * box_edge
    slot_count = old_fields.shape[2]
    box_count = neighbours.shape[1]
    position = lax.axis_index("box")
    counts = old_count[0]
    run_ends = jnp.cumsum(counts)
    run_starts = run_ends - counts
    wanted = position * box_count + jnp.arange(box_count, dtype=jnp.int32)
    source = jnp.sum((run_ends[None, :] <= wanted[:, None]).astype(jnp.int32), axis=1)
    old_slot = wanted - jnp.take(run_starts, source)
    holdings = old_fields[:, 0]
    gathered = with_halo(holdings, (("box", 1),), slot_count)
    moved_fields = jnp.take(gathered, (source - position + 1) * slot_count + old_slot, axis=1)
    solution = moved_fields[0]
    right_side = moved_fields[1]
    coefficient = moved_fields[2]
    link_rows = neighbours[0]
    first_box = position * box_count
    lower_offset = first_box - box_count
    upper_offset = first_box + box_count
    columns = jnp.arange(plane_cells, dtype=jnp.int32)
    depth_ids = columns % box_edge
    low_mask = (depth_ids == 0)[None, None, :]
    high_mask = (depth_ids == box_edge - 1)[None, None, :]
    layer_ids = jnp.arange(box_edge, dtype=jnp.int32)
    parity = (layer_ids[:, None] + columns[None, :] // box_edge + depth_ids[None, :]) % 2
    edge_pair = jnp.stack(
        [
            jnp.concatenate([solution[:, 0], solution[:, box_edge - 1]], axis=0),
            jnp.concatenate([coefficient[:, 0], coefficient[:, box_edge - 1]], axis=0),
        ]
    )
    beside_all = with_halo(edge_pair, (("box", 1),), box_count)
    coef_ghosts = ghost_planes(
        coefficient,
        beside_all[1, :box_count],
        beside_all[1, 3 * box_count :],
        lower_offset,
        upper_offset,
        link_rows,
        first_box,
        True,
        box_edge,
    )
    weights, diagonal = make_weights(coefficient, coef_ghosts, box_edge, low_mask, high_mask)
    lower_faces = beside_all[0, :box_count]
    upper_faces = beside_all[0, 3 * box_count :]
    for sweep_step in range(4):
        if sweep_step > 0:
            lower_faces, upper_faces = fresh_faces(solution, box_count, box_edge)
        ghosts = ghost_planes(
            solution,
            lower_faces,
            upper_faces,
            lower_offset,
            upper_offset,
            link_rows,
            first_box,
            False,
            box_edge,
        )
        solution = half_sweep(
            solution,
            ghosts,
            right_side,
            weights,
            diagonal,
            parity,
            sweep_step % 2,
            box_edge,
            low_mask,
            high_mask,
        )
    lower_faces, upper_faces = fresh_faces(solution, box_count, box_edge)
    final_ghosts = ghost_planes(
        solution,
        lower_faces,
        upper_faces,
        lower_offset,
        upper_offset,
        link_rows,
        first_box,
        False,
        box_edge,
    )
    nearby = beside_cells(solution, final_ghosts, box_edge, low_mask, high_mask)
    residual = right_side - (diagonal * solution - weighted_sum(weights, nearby))
    half_edge = box_edge // 2
    octant_cells = half_edge * half_edge
    paired = residual.reshape(box_count, half_edge, 2, plane_cells).sum(axis=2)
    merge_target = columns // box_edge // 2 * half_edge + depth_ids // 2
    merge_map = (
        merge_target[:, None] == jnp.arange(octant_cells, dtype=jnp.int32)[None, :]
    ).astype(jnp.float32)
    restricted = (
        jnp.einsum("bxm,mq->bxq", paired, merge_map, precision=lax.Precision.HIGHEST) * 0.125
    )
    groups = lax.axis_size("grp")
    owner_group = parents[0, :, 0]
    target_cell = parents[0, :, 1] * 8 + parents[0, :, 2]
    box_ids = jnp.arange(box_count, dtype=jnp.int32)
    earlier = (owner_group[:, None] == owner_group[None, :]) & (box_ids[None, :] < box_ids[:, None])
    send_slot = owner_group * box_count + jnp.sum(earlier.astype(jnp.int32), axis=1)
    placing = (
        send_slot[None, :] == jnp.arange(groups * box_count, dtype=jnp.int32)[:, None]
    ).astype(jnp.float32)
    packed = jnp.dot(placing, restricted.reshape(box_count, -1), precision=lax.Precision.HIGHEST)
    labels = (
        jnp.dot(placing, (target_cell + 1).astype(jnp.float32), precision=lax.Precision.HIGHEST)
        - 1.0
    )
    got_cells, got_labels = (
        lax.all_to_all(
            packed.reshape(groups, box_count, -1), "grp", split_axis=0, concat_axis=0, tiled=True
        ),
        lax.all_to_all(
            labels.reshape(groups, box_count), "grp", split_axis=0, concat_axis=0, tiled=True
        ),
    )
    coarse_slots = coarse_source.shape[1] * 8
    picking = (
        got_labels.reshape(1, -1) == jnp.arange(coarse_slots, dtype=jnp.float32)[:, None]
    ).astype(jnp.float32)
    filled = jnp.dot(
        picking, got_cells.reshape(groups * box_count, -1), precision=lax.Precision.HIGHEST
    )
    covered = jnp.sum(picking, axis=1) > 0.5
    coarse_rhs = jnp.where(
        covered[:, None], filled, coarse_source[0].reshape(coarse_slots, -1)
    ).reshape(coarse_source.shape)
    return (solution[None], residual[None], coarse_rhs)


def solution(mesh):
    in_specs = (
        P(None, "grp", "box", None, None),
        P("grp", None),
        P("grp", "box", None),
        P("grp", "box", None),
        P("grp", "box", None, None, None),
    )
    out_specs = (
        P("grp", "box", None, None),
        P("grp", "box", None, None),
        P("grp", "box", None, None, None),
    )
    return jax.shard_map(
        per_device, mesh=mesh, in_specs=in_specs, out_specs=out_specs, check_vma=False
    )
```

profile of v0, /device:TPU:0, one launch (start us, length us, event | category | flops | bytes accessed | tf_op | source)
XLA Modules:
  0.0 218.9 jit_solution(15206075919034504578)
XLA Ops:
  1.9 6.7 %collective-permute-start = (f32[3,4,32,1024]{3,2,1,0:T(8,128)}, f32[3,4,32,1024]{3,2,1,0:T(8,128)}, u32[]{:S(2)}, u32[]{:S(2)}) collective-permute-start(f32[3,4,32,1024]{3,2,1,0:T(8,128)} %bitcast.225), channel_id=1, source_target_pairs={{0,4},{4,8},{8,12},{12,16},{16,20},{20,24},{24,28},{1,5},{5,9},{9,... | collective-permute-start | bytes 4718600 | tf_op jit(solution)/shard_map/ppermute | solution.py:17
  11.3 3.3 %all-to-all-start = ((f32[4,1,2]{2,1,0:T(1,128)}), f32[4,1,2]{2,1,0:T(1,128)S(1)}, u32[]{:S(2)}, u32[]{:S(2)}) async-start(f32[4,1,2]{2,1,0:T(1,128)} %bitcast.49), calls=%async_computation | async-start | bytes 4096 | tf_op jit(solution)/shard_map/all_to_all | solution.py:227
  19.5 1.8 copy.116
  24.1 16.0 %collective-permute-done.1 = f32[3,4,32,1024]{3,2,1,0:T(8,128)S(1)} collective-permute-done((f32[3,4,32,1024]{3,2,1,0:T(8,128)}, f32[3,4,32,1024]{3,2,1,0:T(8,128)S(1)}, u32[]{:S(2)}, u32[]{:S(2)}) %collective-permute-start.1) | collective-permute-done | bytes 1572896 | tf_op jit(solution)/shard_map/ppermute | solution.py:19
  40.1 34.0 %collective-permute-done = f32[3,4,32,1024]{3,2,1,0:T(8,128)} collective-permute-done((f32[3,4,32,1024]{3,2,1,0:T(8,128)}, f32[3,4,32,1024]{3,2,1,0:T(8,128)}, u32[]{:S(2)}, u32[]{:S(2)}) %collective-permute-start) | collective-permute-done | bytes 1572896 | tf_op jit(solution)/shard_map/ppermute | solution.py:17
  74.0 4.8 %pad_maximum_fusion = f32[3,12,32,1024]{3,2,1,0:T(8,128)} fusion(f32[3,4,32,1024]{3,2,1,0:T(8,128)S(1)} %collective-permute-done.1, f32[3,4,32,1024]{3,2,1,0:T(8,128)} %bitcast.226, f32[3,4,32,1024]{3,2,1,0:T(8,128)} %collective-permute-done), kind=kLoop, calls=%fused_computation.38 | loop fusion | flops 2359296 | bytes 9437184 | tf_op jit(solution)/shard_map/concatenate | solution.py:15
  78.8 2.9 %gather_fusion.1 = f32[2,3,32,1024]{3,2,1,0:T(8,128)S(1)} fusion(f32[3,12,32,1024]{3,2,1,0:T(8,128)} %pad_maximum_fusion, s32[1024]{0:T(1024)S(1)} %pad_clamp_fusion.6), kind=kCustom, calls=%fused_computation.37 | custom fusion | bytes 1572872 | tf_op jit(solution)/shard_map/jit(_take)/gather | solution.py:124
  86.9 4.4 %collective-permute-start.2 = (f32[2,2,1024]{2,1,0:T(2,128)S(1)}, f32[2,2,1024]{2,1,0:T(2,128)S(1)}, u32[]{:S(2)}, u32[]{:S(2)}) collective-permute-start(f32[2,2,1024]{2,1,0:T(2,128)S(1)} %get-tuple-element.99), channel_id=1, source_target_pairs={{0,4},{4,8},{8,12},{12,16},{16,20},{20,24},{24,28},{1,5},{5,9},{9,... | collective-permute-start | bytes 49160 | tf_op jit(solution)/shard_map/ppermute | solution.py:17
  104.7 2.6 %fusion.12 = (f32[2,32,1024]{2,1,0:T(8,128)S(1)}, f32[2,32,1024]{2,1,0:T(8,128)S(1)}, f32[2,32,1024]{2,1,0:T(8,128)S(1)}, f32[2,32,1024]{2,1,0:T(8,128)S(1)}, f3...) fusion(f32[2,31,1024]{2,1,0:T(8,128)} %get-tuple-element.127, ...), kind=kLoop, calls=%fused_computation.60 | loop fusion | flops 2883584 | bytes 6849536 | tf_op jit(solution)/shard_map/jit(_where)/select_n | solution.py:101
  110.7 4.5 %collective-permute-start.4 = (f32[2,1024]{1,0:T(2,128)S(1)}, f32[2,1024]{1,0:T(2,128)S(1)}, u32[]{:S(2)}, u32[]{:S(2)}) collective-permute-start(f32[2,1024]{1,0:T(2,128)S(1)} %bitcast.241), channel_id=1, source_target_pairs={{0,4},{4,8},{8,12},{12,16},{16,20},{20,24},{24,28},{1,5},{5,9},{9,... | collective-permute-start | bytes 24584 | tf_op jit(solution)/shard_map/ppermute | solution.py:17
  123.5 1.7 reshape.423
  126.5 1.7 reshape.422
  129.9 1.8 fusion.23
  135.1 4.5 %collective-permute-start.6 = (f32[2,1024]{1,0:T(2,128)S(1)}, f32[2,1024]{1,0:T(2,128)S(1)}, u32[]{:S(2)}, u32[]{:S(2)}) collective-permute-start(f32[2,1024]{1,0:T(2,128)S(1)} %bitcast.242), channel_id=1, source_target_pairs={{0,4},{4,8},{8,12},{12,16},{16,20},{20,24},{24,28},{1,5},{5,9},{9,... | collective-permute-start | bytes 24584 | tf_op jit(solution)/shard_map/ppermute | solution.py:17
  148.0 1.7 reshape.425
  154.4 1.8 fusion.31
  159.6 4.9 %collective-permute-start.8 = (f32[2,1024]{1,0:T(2,128)S(1)}, f32[2,1024]{1,0:T(2,128)S(1)}, u32[]{:S(2)}, u32[]{:S(2)}) collective-permute-start(f32[2,1024]{1,0:T(2,128)S(1)} %bitcast.243), channel_id=1, source_target_pairs={{0,4},{4,8},{8,12},{12,16},{16,20},{20,24},{24,28},{1,5},{5,9},{9,... | collective-permute-start | bytes 24584 | tf_op jit(solution)/shard_map/ppermute | solution.py:17
  175.8 1.7 reshape.426
  179.1 1.8 fusion.39
  184.4 5.4 %collective-permute-start.10 = (f32[2,1024]{1,0:T(2,128)S(1)}, f32[2,1024]{1,0:T(2,128)S(1)}, u32[]{:S(2)}, u32[]{:S(2)}) collective-permute-start(f32[2,1024]{1,0:T(2,128)S(1)} %bitcast.237), channel_id=1, source_target_pairs={{0,4},{4,8},{8,12},{12,16},{16,20},{20,24},{24,28},{1,5},{5,9},{9,... | collective-permute-start | bytes 24584 | tf_op jit(solution)/shard_map/ppermute | solution.py:17
  197.9 1.7 reshape.429
  204.3 2.5 %fusion.46 = f32[2,32,1024]{2,1,0:T(8,128)} fusion(f32[2,32,1024]{2,1,0:T(8,128)S(1)} %get-tuple-element.23, f32[2,31,1024]{2,1,0:T(8,128)} %get-tuple-element.45, f32[2,1,1024]{2,1,0:T(1,128)S(1)} %copy.90, f32[2,32,1024]{2,1,0:T(8,128)S(1)} %get-tuple-element.22, f32[2,1,1024]{2,1,0:T(1,128)S(1)} %broadcast_in_dim.373, ...), kind=kLoop, calls=%fused_computation.113 | loop fusion | flops 1703936 | bytes 4457984 | tf_op jit(solution)/shard_map/sub | solution.py:198
  209.7 3.3 %all-to-all-start.1 = ((f32[4,2,4096]{2,1,0:T(2,128)}), f32[4,2,4096]{2,1,0:T(2,128)S(1)}, u32[]{:S(2)}, u32[]{:S(2)}) async-start(f32[4,2,4096]{2,1,0:T(2,128)} %fusion.121), calls=%async_computation.1 | async-start | bytes 262144 | tf_op jit(solution)/shard_map/all_to_all | solution.py:224
  213.1 4.6 %all-to-all-done.1 = f32[4,2,4096]{2,1,0:T(2,128)S(1)} async-done(((f32[4,2,4096]{2,1,0:T(2,128)}), f32[4,2,4096]{2,1,0:T(2,128)S(1)}, u32[]{:S(2)}, u32[]{:S(2)}) %all-to-all-start.1) | async-done | bytes 131104 | tf_op jit(solution)/shard_map/all_to_all | solution.py:224
  (320 shorter events, 96.6 us)
Async XLA Ops:
  0.6 39.4 %collective-permute-start.1 = (f32[3,4,32,1024]{3,2,1,0:T(8,128)}, f32[3,4,32,1024]{3,2,1,0:T(8,128)S(1)}, u32[]{:S(2)}, u32[]{:S(2)}) collective-permute-start(f32[3,4,32,1024]{3,2,1,0:T(8,128)} %bitcast.224), channel_id=1, source_target_pairs={{4,0},{8,4},{12,8},{16,12},{20,16},{24,20},{28,24},{5,1},{9,5},{13... | collective-permute-start | bytes 4718600 | tf_op jit(solution)/shard_map/ppermute | solution.py:19
  1.9 72.1 %collective-permute-start = (f32[3,4,32,1024]{3,2,1,0:T(8,128)}, f32[3,4,32,1024]{3,2,1,0:T(8,128)}, u32[]{:S(2)}, u32[]{:S(2)}) collective-permute-start(f32[3,4,32,1024]{3,2,1,0:T(8,128)} %bitcast.225), channel_id=1, source_target_pairs={{0,4},{4,8},{8,12},{12,16},{16,20},{20,24},{24,28},{1,5},{5,9},{9,... | collective-permute-start | bytes 4718600 | tf_op jit(solution)/shard_map/ppermute | solution.py:17
  11.3 10.9 %all-to-all-start = ((f32[4,1,2]{2,1,0:T(1,128)}), f32[4,1,2]{2,1,0:T(1,128)S(1)}, u32[]{:S(2)}, u32[]{:S(2)}) async-start(f32[4,1,2]{2,1,0:T(1,128)} %bitcast.49), calls=%async_computation | async-start | bytes 4096 | tf_op jit(solution)/shard_map/all_to_all | solution.py:227
  18.7 84.6 %copy-start.29 = (pred[2]{0:T(512)(128)(4,1)}, pred[2]{0:T(512)(128)(4,1)S(1)}, u32[]{:S(2)}) copy-start(pred[2]{0:T(512)(128)(4,1)S(1)} %compare_bitcast_fusion.5) | copy-start | bytes 10
  18.7 84.6 %copy-start.15 = (pred[2]{0:T(512)(128)(4,1)}, pred[2]{0:T(512)(128)(4,1)S(1)}, u32[]{:S(2)}) copy-start(pred[2]{0:T(512)(128)(4,1)S(1)} %get-tuple-element.34) | copy-start | bytes 10
  18.7 84.0 %copy-start.35 = (s32[1024]{0:T(1024)}, s32[1024]{0:T(1024)S(1)}, u32[]{:S(2)}) copy-start(s32[1024]{0:T(1024)S(1)} %pad_clamp_fusion.5) | copy-start | bytes 12292
  18.8 85.7 %copy-start.24 = (pred[2]{0:T(512)(128)(4,1)}, pred[2]{0:T(512)(128)(4,1)S(1)}, u32[]{:S(2)}) copy-start(pred[2]{0:T(512)(128)(4,1)S(1)} %compare_bitcast_fusion.4) | copy-start | bytes 10
  18.8 85.7 %copy-start.10 = (pred[2]{0:T(512)(128)(4,1)}, pred[2]{0:T(512)(128)(4,1)S(1)}, u32[]{:S(2)}) copy-start(pred[2]{0:T(512)(128)(4,1)S(1)} %get-tuple-element.32) | copy-start | bytes 10
  18.9 85.1 %copy-start.34 = (s32[1024]{0:T(1024)}, s32[1024]{0:T(1024)S(1)}, u32[]{:S(2)}) copy-start(s32[1024]{0:T(1024)S(1)} %pad_clamp_fusion.4) | copy-start | bytes 12292
  19.1 78.7 %copy-start.2 = (pred[2]{0:T(512)(128)(4,1)}, pred[2]{0:T(512)(128)(4,1)S(1)}, u32[]{:S(2)}) copy-start(pred[2]{0:T(512)(128)(4,1)S(1)} %get-tuple-element.28) | copy-start | bytes 10
  19.3 78.6 %copy-start.6 = (pred[2]{0:T(512)(128)(4,1)}, pred[2]{0:T(512)(128)(4,1)S(1)}, u32[]{:S(2)}) copy-start(pred[2]{0:T(512)(128)(4,1)S(1)} %get-tuple-element.26) | copy-start | bytes 10
  19.3 78.7 %copy-start.4 = (pred[2]{0:T(512)(128)(4,1)}, pred[2]{0:T(512)(128)(4,1)S(1)}, u32[]{:S(2)}) copy-start(pred[2]{0:T(512)(128)(4,1)S(1)} %get-tuple-element.123) | copy-start | bytes 10
  19.4 77.9 %copy-start.37 = (s32[1024]{0:T(1024)}, s32[1024]{0:T(1024)S(1)}, u32[]{:S(2)}) copy-start(s32[1024]{0:T(1024)S(1)} %pad_clamp_fusion.1) | copy-start | bytes 12292
  86.9 15.2 %collective-permute-start.2 = (f32[2,2,1024]{2,1,0:T(2,128)S(1)}, f32[2,2,1024]{2,1,0:T(2,128)S(1)}, u32[]{:S(2)}, u32[]{:S(2)}) collective-permute-start(f32[2,2,1024]{2,1,0:T(2,128)S(1)} %get-tuple-element.99), channel_id=1, source_target_pairs={{0,4},{4,8},{8,12},{12,16},{16,20},{20,24},{24,28},{1,5},{5,9},{9,... | collective-permute-start | bytes 49160 | tf_op jit(solution)/shard_map/ppermute | solution.py:17
  91.3 12.1 %collective-permute-start.3 = (f32[2,2,1024]{2,1,0:T(2,128)S(1)}, f32[2,2,1024]{2,1,0:T(2,128)S(1)}, u32[]{:S(2)}, u32[]{:S(2)}) collective-permute-start(f32[2,2,1024]{2,1,0:T(2,128)S(1)} %get-tuple-element.98), channel_id=1, source_target_pairs={{4,0},{8,4},{12,8},{16,12},{20,16},{24,20},{28,24},{5,1},{9,5},{13... | collective-permute-start | bytes 49160 | tf_op jit(solution)/shard_map/ppermute | solution.py:19
  110.7 17.5 %collective-permute-start.4 = (f32[2,1024]{1,0:T(2,128)S(1)}, f32[2,1024]{1,0:T(2,128)S(1)}, u32[]{:S(2)}, u32[]{:S(2)}) collective-permute-start(f32[2,1024]{1,0:T(2,128)S(1)} %bitcast.241), channel_id=1, source_target_pairs={{0,4},{4,8},{8,12},{12,16},{16,20},{20,24},{24,28},{1,5},{5,9},{9,... | collective-permute-start | bytes 24584 | tf_op jit(solution)/shard_map/ppermute | solution.py:17
  115.3 13.8 %collective-permute-start.5 = (f32[2,1024]{1,0:T(2,128)S(1)}, f32[2,1024]{1,0:T(2,128)S(1)}, u32[]{:S(2)}, u32[]{:S(2)}) collective-permute-start(f32[2,1024]{1,0:T(2,128)S(1)} %bitcast.238), channel_id=1, source_target_pairs={{4,0},{8,4},{12,8},{16,12},{20,16},{24,20},{28,24},{5,1},{9,5},{13... | collective-permute-start | bytes 24584 | tf_op jit(solution)/shard_map/ppermute | solution.py:19
  135.1 17.7 %collective-permute-start.6 = (f32[2,1024]{1,0:T(2,128)S(1)}, f32[2,1024]{1,0:T(2,128)S(1)}, u32[]{:S(2)}, u32[]{:S(2)}) collective-permute-start(f32[2,1024]{1,0:T(2,128)S(1)} %bitcast.242), channel_id=1, source_target_pairs={{0,4},{4,8},{8,12},{12,16},{16,20},{20,24},{24,28},{1,5},{5,9},{9,... | collective-permute-start | bytes 24584 | tf_op jit(solution)/shard_map/ppermute | solution.py:17
  139.6 13.9 %collective-permute-start.7 = (f32[2,1024]{1,0:T(2,128)S(1)}, f32[2,1024]{1,0:T(2,128)S(1)}, u32[]{:S(2)}, u32[]{:S(2)}) collective-permute-start(f32[2,1024]{1,0:T(2,128)S(1)} %bitcast.239), channel_id=1, source_target_pairs={{4,0},{8,4},{12,8},{16,12},{20,16},{24,20},{28,24},{5,1},{9,5},{13... | collective-permute-start | bytes 24584 | tf_op jit(solution)/shard_map/ppermute | solution.py:19
  159.6 17.9 %collective-permute-start.8 = (f32[2,1024]{1,0:T(2,128)S(1)}, f32[2,1024]{1,0:T(2,128)S(1)}, u32[]{:S(2)}, u32[]{:S(2)}) collective-permute-start(f32[2,1024]{1,0:T(2,128)S(1)} %bitcast.243), channel_id=1, source_target_pairs={{0,4},{4,8},{8,12},{12,16},{16,20},{20,24},{24,28},{1,5},{5,9},{9,... | collective-permute-start | bytes 24584 | tf_op jit(solution)/shard_map/ppermute | solution.py:17
  164.5 13.8 %collective-permute-start.9 = (f32[2,1024]{1,0:T(2,128)S(1)}, f32[2,1024]{1,0:T(2,128)S(1)}, u32[]{:S(2)}, u32[]{:S(2)}) collective-permute-start(f32[2,1024]{1,0:T(2,128)S(1)} %bitcast.240), channel_id=1, source_target_pairs={{4,0},{8,4},{12,8},{16,12},{20,16},{24,20},{28,24},{5,1},{9,5},{13... | collective-permute-start | bytes 24584 | tf_op jit(solution)/shard_map/ppermute | solution.py:19
  184.4 18.3 %collective-permute-start.10 = (f32[2,1024]{1,0:T(2,128)S(1)}, f32[2,1024]{1,0:T(2,128)S(1)}, u32[]{:S(2)}, u32[]{:S(2)}) collective-permute-start(f32[2,1024]{1,0:T(2,128)S(1)} %bitcast.237), channel_id=1, source_target_pairs={{0,4},{4,8},{8,12},{12,16},{16,20},{20,24},{24,28},{1,5},{5,9},{9,... | collective-permute-start | bytes 24584 | tf_op jit(solution)/shard_map/ppermute | solution.py:17
  189.8 13.7 %collective-permute-start.11 = (f32[2,1024]{1,0:T(2,128)S(1)}, f32[2,1024]{1,0:T(2,128)S(1)}, u32[]{:S(2)}, u32[]{:S(2)}) collective-permute-start(f32[2,1024]{1,0:T(2,128)S(1)} %bitcast.236), channel_id=1, source_target_pairs={{4,0},{8,4},{12,8},{16,12},{20,16},{24,20},{28,24},{5,1},{9,5},{13... | collective-permute-start | bytes 24584 | tf_op jit(solution)/shard_map/ppermute | solution.py:19
  209.7 7.9 %all-to-all-start.1 = ((f32[4,2,4096]{2,1,0:T(2,128)}), f32[4,2,4096]{2,1,0:T(2,128)S(1)}, u32[]{:S(2)}, u32[]{:S(2)}) async-start(f32[4,2,4096]{2,1,0:T(2,128)} %fusion.121), calls=%async_computation.1 | async-start | bytes 262144 | tf_op jit(solution)/shard_map/all_to_all | solution.py:224
  (35 other events, 1182.9 us)
where the time goes:
time: 222 us; the launch traced here: 219 us
  local copies, waits for them, and re-layouts  81.6 us (37%)
  waiting for transfers between devices  54.5 us (25%)
  starting transfers between devices  45.1 us (20%)
  other arithmetic  33.8 us (15%)
    ppermute x6, waiting for transfers between devices, with_halo(): lax.ppermute(tail, axis, [(i, (i + 1) % count) for i in range(ends)])  34 us
    ppermute x6, starting transfers between devices, with_halo(): lax.ppermute(tail, axis, [(i, (i + 1) % count) for i in range(ends)])  30.5 us
    gather x36, local copies, waits for them, and re-layouts, ghost_planes(): chosen = jnp.take(tables[face_id], local_row, axis=0)  22.9 us
    ppermute x6, waiting for transfers between devices, with_halo(): lax.ppermute(head, axis, [((i + 1) % count, i) for i in range(ends)])  16 us
    select_n x21, other arithmetic, ghost_planes(): results.append(jnp.where(is_valid, chosen, fallback))  12.2 us
    reshape x6, local copies, waits for them, and re-layouts, beside_cells(): jnp.repeat(planes[5], box_edge, axis=2)  8.54 us
    select_n x4, other arithmetic, half_sweep(): return jnp.where(parity_rows == colour, updated, field)  8.09 us
    ppermute x6, starting transfers between devices, with_halo(): lax.ppermute(head, axis, [((i + 1) % count, i) for i in range(ends)])  7.93 us
  transfers between devices with their start and end apart: 14, of which 3 were waited for; matrix products, arithmetic and copies ran while one was open for 33% of the time, Pallas kernels for 0%

commit v1 on v0

v1 whole, which is shorter than its diff:
```python
import jax
import jax.numpy as jnp
from jax import lax
from jax.experimental import pallas as pl
from jax.experimental.pallas import tpu as pltpu
from jax.sharding import PartitionSpec as P

MASS_TERM = 0.25
MESH = pl.DeviceIdType.MESH
LANES = 128
TILE = 8
PAD = 8
FACES = 6


def level_kernel(
    old_ref,
    count_ref,
    link_ref,
    parent_ref,
    coarse_ref,
    smooth_out,
    residual_out,
    coarse_out,
    held_sol,
    held_rhs,
    held_coef,
    send_right,
    sol,
    coef,
    weights,
    diagonal,
    scaled_rhs,
    plane_out,
    res_rows,
    merge_map,
    merged,
    pack,
    got_pack,
    coarse_buf,
    face_out,
    face_in,
    load_sem,
    move_send,
    move_recv,
    face_send,
    face_recv,
    pack_send,
    pack_recv,
    store_sem,
):
    place = lax.axis_index("box")
    group = lax.axis_index("grp")
    curve = lax.axis_size("box")
    groups = lax.axis_size("grp")
    slots = old_ref.shape[2]
    boxes = link_ref.shape[1]
    edge = old_ref.shape[3]
    cells = old_ref.shape[4]
    tiles = edge // TILE
    columns = cells // LANES
    half = edge // 2
    coarse_slots = coarse_buf.shape[0]
    has_left = place > 0
    has_right = place < curve - 1
    held = (held_sol, held_rhs, held_coef)

    def load(field):
        return pltpu.make_async_copy(
            old_ref.at[field, 0], held[field].at[pl.ds(0, slots)], load_sem.at[field]
        )

    coarse_load = pltpu.make_async_copy(coarse_ref, coarse_buf, load_sem.at[3])
    for field in (2, 0, 1):
        load(field).start()
    coarse_load.start()

    barrier = pltpu.get_barrier_semaphore()

    @pl.when(has_left)
    def _():
        pl.semaphore_signal(barrier, inc=1, device_id=(place - 1, group), device_id_type=MESH)

    @pl.when(has_right)
    def _():
        pl.semaphore_signal(barrier, inc=1, device_id=(place + 1, group), device_id_type=MESH)

    for step in range(1, groups):
        pl.semaphore_signal(
            barrier,
            inc=1,
            device_id=(place, lax.rem(group + step, groups)),
            device_id_type=MESH,
        )
    pl.semaphore_wait(
        barrier, groups - 1 + has_left.astype(jnp.int32) + has_right.astype(jnp.int32)
    )

    def move_left(field):
        return pltpu.make_async_remote_copy(
            src_ref=old_ref.at[field, 0, 0],
            dst_ref=held[field].at[slots + 1],
            send_sem=move_send.at[0, field],
            recv_sem=move_recv.at[0, field],
            device_id=(place - 1, group),
            device_id_type=MESH,
        )

    def move_right(field):
        return pltpu.make_async_remote_copy(
            src_ref=send_right.at[field],
            dst_ref=held[field].at[slots],
            send_sem=move_send.at[1, field],
            recv_sem=move_recv.at[1, field],
            device_id=(place + 1, group),
            device_id_type=MESH,
        )

    start = jnp.int32(0)
    for other in range(curve):
        start = start + jnp.where(other < place, count_ref[0, other], 0)
    end = start
    for other in range(curve):
        end = end + jnp.where(other == place, count_ref[0, other], 0)
    first = place * boxes
    right_slot = jnp.clip(first + boxes - start, 0, slots - 1)
    own_rows = []
    for b in range(boxes):
        wanted = first + b
        own = jnp.clip(wanted - start, 0, slots - 1)
        own_rows.append(
            jnp.where(wanted < start, slots, jnp.where(wanted >= end, slots + 1, own))
        )

    for field in (2, 0, 1):

        @pl.when(has_left)
        def _(field=field):
            move_left(field).start()

        load(field).wait()
        chosen = held[field][0]
        for s in range(1, slots):
            chosen = jnp.where(right_slot == s, held[field][s], chosen)
        send_right[field] = chosen

        @pl.when(has_right)
        def _(field=field):
            move_right(field).start()

    def move_wait(field):
        @pl.when(has_right)
        def _():
            move_left(field).wait_recv()

        @pl.when(has_left)
        def _():
            move_right(field).wait_recv()

    def face_to(k, side):
        return pltpu.make_async_remote_copy(
            src_ref=face_out.at[k, side],
            dst_ref=face_in.at[k, side],
            send_sem=face_send.at[k, side],
            recv_sem=face_recv.at[k, side],
            device_id=(place + 2 * side - 1, group),
            device_id_type=MESH,
        )

    def faces_start(k, ref):
        for b in range(boxes):
            face_out[k, 0, b] = ref[b, :, PAD : PAD + 1, :]
            face_out[k, 1, b] = ref[b, :, PAD + edge - 1 : PAD + edge, :]

        @pl.when(has_left)
        def _():
            face_to(k, 0).start()

        @pl.when(has_right)
        def _():
            face_to(k, 1).start()

    def faces_wait(k):
        @pl.when(has_left)
        def _():
            face_to(k, 1).wait_recv()

        @pl.when(has_right)
        def _():
            face_to(k, 0).wait_recv()

    links = [[link_ref[0, b, f] for f in range(FACES)] for b in range(boxes)]
    linked = [[jnp.where(t >= 0, 1.0, 0.0) for t in row] for row in links]
    beside = [[jnp.clip(t - first, 0, boxes - 1) for t in row] for row in links]

    def ghost_rows(k, ref, keep_own):
        for b in range(boxes):
            for f, side, base, row, own in (
                (0, 1, first - boxes, PAD - 1, PAD),
                (1, 0, first + boxes, PAD + edge, PAD + edge - 1),
            ):
                if keep_own:
                    plane = ref[b, :, own : own + 1, :]
                else:
                    plane = jnp.zeros((columns, 1, LANES), jnp.float32)
                for other in range(boxes):
                    plane = jnp.where(
                        (links[b][f] >= 0) & (links[b][f] == base + other),
                        face_in[k, side, other],
                        plane,
                    )
                ref[b, :, row : row + 1, :] = plane

    shape = (columns, TILE, LANES)
    lane = lax.broadcasted_iota(jnp.int32, shape, 2)
    column = lax.broadcasted_iota(jnp.int32, shape, 0)
    depth = lane & (edge - 1)
    low_depth = depth == 0
    high_depth = depth == edge - 1
    low_lane = lane < edge
    high_lane = lane >= LANES - edge
    low_row = low_lane & (column == 0)
    high_row = high_lane & (column == columns - 1)
    edge_masks = (None, None, low_row, high_row, low_depth, high_depth)
    parity = (
        lax.broadcasted_iota(jnp.int32, shape, 1)
        + column * (LANES // edge)
        + (lane >> (edge.bit_length() - 1))
        + depth
    ) & 1

    def around(ref, b, t):
        rows = slice(PAD + t * TILE, PAD + (t + 1) * TILE)
        here = ref[b, :, rows, :]
        low_y = pltpu.roll(here, edge, 2)
        high_y = pltpu.roll(here, LANES - edge, 2)
        ghost_low = pltpu.roll(ref[beside[b][2], columns - 1, rows, :], edge, 1)
        ghost_high = pltpu.roll(ref[beside[b][3], 0, rows, :], LANES - edge, 1)
        before = jnp.concatenate([ghost_low[None], low_y[:-1]], axis=0)
        after = jnp.concatenate([high_y[1:], ghost_high[None]], axis=0)
        return here, (
            ref[b, :, PAD + t * TILE - 1 : PAD + (t + 1) * TILE - 1, :],
            ref[b, :, PAD + t * TILE + 1 : PAD + (t + 1) * TILE + 1, :],
            jnp.where(low_lane, before, low_y),
            jnp.where(high_lane, after, high_y),
            jnp.where(
                low_depth,
                pltpu.roll(ref[beside[b][4], :, rows, :], LANES - edge + 1, 2),
                pltpu.roll(here, 1, 2),
            ),
            jnp.where(
                high_depth,
                pltpu.roll(ref[beside[b][5], :, rows, :], edge - 1, 2),
                pltpu.roll(here, LANES - 1, 2),
            ),
        )

    def spread(rows):
        return jnp.stack([rows[:, c * LANES : (c + 1) * LANES] for c in range(columns)])

    def flatten(block):
        return jnp.concatenate([block[c] for c in range(columns)], axis=1)

    target = lax.broadcasted_iota(jnp.int32, merge_map.shape, 0)
    target = ((target >> edge.bit_length()) * half) + (
        (target & (edge - 1)) >> 1
    )
    merge_map[...] = jnp.where(
        target == lax.broadcasted_iota(jnp.int32, merge_map.shape, 1), 1.0, 0.0
    ).astype(jnp.bfloat16)
    for b in range(boxes):
        label = (
            parent_ref[0, b, 0] * coarse_slots + parent_ref[0, b, 1] * 8 + parent_ref[0, b, 2]
        ).astype(jnp.float32)
        pack[b, half : half + TILE, :] = jnp.full((TILE, half * half), label, jnp.float32)

    def take(field, ref):
        for b in range(boxes):
            for t in range(tiles):
                ref[b, :, PAD + t * TILE : PAD + (t + 1) * TILE, :] = spread(
                    held[field][own_rows[b], t * TILE : (t + 1) * TILE, :]
                )

    move_wait(2)
    take(2, coef)
    faces_start(0, coef)
    move_wait(0)
    take(0, sol)
    faces_start(1, sol)
    faces_wait(0)
    ghost_rows(0, coef, True)
    for b in range(boxes):
        for t in range(tiles):
            here, near = around(coef, b, t)
            total = jnp.full(shape, MASS_TERM, jnp.float32)
            kept = []
            for f in range(FACES):
                beyond = near[f]
                if f >= 2:
                    inside = linked[b][f]
                    beyond = jnp.where(
                        edge_masks[f], beyond * inside + here * (1.0 - inside), beyond
                    )
                weight = 0.5 * (here + beyond)
                total = total + weight
                if f >= 2:
                    weight = jnp.where(edge_masks[f], weight * linked[b][f], weight)
                kept.append(weight)
            inverse = 1.0 / total
            diagonal[b, t] = total
            scaled_rhs[b, t] = inverse
            for f in range(FACES):
                weights[b, t, f] = kept[f] * inverse

    move_wait(1)
    for b in range(boxes):
        for t in range(tiles):
            scaled_rhs[b, t] = scaled_rhs[b, t] * spread(
                held[1][own_rows[b], t * TILE : (t + 1) * TILE, :]
            )

    def relaxed(b, t):
        here, near = around(sol, b, t)
        total = scaled_rhs[b, t]
        for f in range(FACES):
            total = total + weights[b, t, f] * near[f]
        return here, total

    inner = list(range(1, tiles - 1))
    outer = [0, tiles - 1] if tiles > 1 else [0]

    def sweep(colour, which):
        for b in range(boxes):
            for t in which:
                here, total = relaxed(b, t)
                sol[b, :, PAD + t * TILE : PAD + (t + 1) * TILE, :] = jnp.where(
                    parity == colour, total, here
                )

    for step in range(4):
        sweep(step % 2, inner)
        faces_wait(step + 1)
        ghost_rows(step + 1, sol, False)
        sweep(step % 2, outer)
        faces_start(step + 2, sol)

    for b in range(boxes):
        for t in range(tiles):
            plane_out[b, t * TILE : (t + 1) * TILE, :] = flatten(
                sol[b, :, PAD + t * TILE : PAD + (t + 1) * TILE, :]
            )
    smooth_store = pltpu.make_async_copy(plane_out, smooth_out.at[0], store_sem.at[0])
    smooth_store.start()

    def leave(which):
        for b in range(boxes):
            for t in which:
                here, total = relaxed(b, t)
                res_rows[b, t * TILE : (t + 1) * TILE, :] = flatten(
                    diagonal[b, t] * (total - here)
                )

    leave(inner)
    faces_wait(5)
    ghost_rows(5, sol, False)
    leave(outer)
    residual_store = pltpu.make_async_copy(res_rows, residual_out.at[0], store_sem.at[1])
    residual_store.start()

    for b in range(boxes):
        rows = res_rows[b]
        high = rows.astype(jnp.bfloat16)
        low = (rows - high.astype(jnp.float32)).astype(jnp.bfloat16)
        both = jnp.dot(
            jnp.concatenate([high, low], axis=0),
            merge_map[...],
            preferred_element_type=jnp.float32,
        )
        both = both[:edge] + both[edge:]
        for c in range(merged.shape[1]):
            merged[b, c] = both[:, c * LANES : (c + 1) * LANES]
    for b in range(boxes):
        for c in range(merged.shape[1]):
            pack[b, 0:half, c * LANES : (c + 1) * LANES] = 0.125 * (
                merged[b, c, pl.ds(0, half, stride=2), :]
                + merged[b, c, pl.ds(1, half, stride=2), :]
            )

    def pack_to(step):
        return pltpu.make_async_remote_copy(
            src_ref=pack,
            dst_ref=got_pack.at[step - 1],
            send_sem=pack_send.at[step - 1],
            recv_sem=pack_recv.at[step - 1],
            device_id=(place, lax.rem(group + step, groups)),
            device_id_type=MESH,
        )

    for step in range(1, groups):
        pack_to(step).start()
    coarse_load.wait()

    def place_from(refs):
        for ref in refs:
            for b in range(boxes):
                label = ref[b, half : half + TILE, :]
                label = jnp.concatenate([label] * (half // TILE), axis=0)
                values = ref[b, 0:half, :]

                def put(s, carry, label=label, values=values):
                    mine = (group * coarse_slots + s).astype(jnp.float32)
                    coarse_buf[s] = jnp.where(label == mine, values, coarse_buf[s])
                    return carry

                lax.fori_loop(0, coarse_slots, put, 0, unroll=True)

    place_from([pack])
    for step in range(1, groups):
        pack_to(step).wait_recv()
        place_from([got_pack.at[step - 1]])
    coarse_store = pltpu.make_async_copy(coarse_buf, coarse_out, store_sem.at[2])
    coarse_store.start()

    for step in range(1, groups):
        pack_to(step).wait_send()

    @pl.when(has_left)
    def _():
        for field in range(3):
            move_left(field).wait_send()
        for k in range(6):
            face_to(k, 0).wait_send()

    @pl.when(has_right)
    def _():
        for field in range(3):
            move_right(field).wait_send()
        for k in range(6):
            face_to(k, 1).wait_send()

    smooth_store.wait()
    residual_store.wait()
    coarse_store.wait()


def per_device(old_fields, old_count, neighbours, parents, coarse_source):
    fields, _, slots, edge, cells = old_fields.shape
    boxes = neighbours.shape[1]
    groups = lax.axis_size("grp")
    _, coarse_boxes, octants, half, quarter = coarse_source.shape
    tiles = edge // TILE
    columns = cells // LANES
    padded = edge + 2 * PAD
    f32 = jnp.float32
    coarse_slots = coarse_boxes * octants
    scratch = [
        pltpu.VMEM((slots + 2, edge, cells), f32),
        pltpu.VMEM((slots + 2, edge, cells), f32),
        pltpu.VMEM((slots + 2, edge, cells), f32),
        pltpu.VMEM((fields, edge, cells), f32),
        pltpu.VMEM((boxes, columns, padded, LANES), f32),
        pltpu.VMEM((boxes, columns, padded, LANES), f32),
        pltpu.VMEM((boxes, tiles, FACES, columns, TILE, LANES), f32),
        pltpu.VMEM((boxes, tiles, columns, TILE, LANES), f32),
        pltpu.VMEM((boxes, tiles, columns, TILE, LANES), f32),
        pltpu.VMEM((boxes, edge, cells), f32),
        pltpu.VMEM((boxes, edge, cells), f32),
        pltpu.VMEM((cells, quarter), jnp.bfloat16),
        pltpu.VMEM((boxes, quarter // LANES, edge, LANES), f32),
        pltpu.VMEM((boxes, half + TILE, quarter), f32),
        pltpu.VMEM((groups - 1, boxes, half + TILE, quarter), f32),
        pltpu.VMEM((coarse_slots, half, quarter), f32),
        pltpu.VMEM((6, 2, boxes, columns, 1, LANES), f32),
        pltpu.VMEM((6, 2, boxes, columns, 1, LANES), f32),
        pltpu.SemaphoreType.DMA((4,)),
        pltpu.SemaphoreType.DMA((2, 3)),
        pltpu.SemaphoreType.DMA((2, 3)),
        pltpu.SemaphoreType.DMA((6, 2)),
        pltpu.SemaphoreType.DMA((6, 2)),
        pltpu.SemaphoreType.DMA((groups - 1,)),
        pltpu.SemaphoreType.DMA((groups - 1,)),
        pltpu.SemaphoreType.DMA((3,)),
    ]
    anywhere = pl.BlockSpec(memory_space=pl.ANY)
    scalars = pl.BlockSpec(memory_space=pltpu.SMEM)
    smoothed, residual, coarse_rhs = pl.pallas_call(
        level_kernel,
        out_shape=(
            jax.ShapeDtypeStruct((1, boxes, edge, cells), f32),
            jax.ShapeDtypeStruct((1, boxes, edge, cells), f32),
            jax.ShapeDtypeStruct((coarse_slots, half, quarter), f32),
        ),
        in_specs=[anywhere, scalars, scalars, scalars, anywhere],
        out_specs=(anywhere, anywhere, anywhere),
        scratch_shapes=scratch,
        compiler_params=pltpu.CompilerParams(
            collective_id=0, has_side_effects=True, vmem_limit_bytes=48 * 1024 * 1024
        ),
    )(
        old_fields,
        old_count,
        neighbours,
        parents,
        coarse_source.reshape(coarse_slots, half, quarter),
    )
    return smoothed, residual, coarse_rhs.reshape(coarse_source.shape)


def solution(mesh):
    in_specs = (
        P(None, "grp", "box", None, None),
        P("grp", None),
        P("grp", "box", None),
        P("grp", "box", None),
        P("grp", "box", None, None, None),
    )
    out_specs = (
        P("grp", "box", None, None),
        P("grp", "box", None, None),
        P("grp", "box", None, None, None),
    )
    return jax.shard_map(
        per_device, mesh=mesh, in_specs=in_specs, out_specs=out_specs, check_vma=False
    )
```

time: 222 us -> 50.5 us (0.23); the launches traced: 219 us -> 50.3 us
  local copies, waits for them, and re-layouts: 81.6 us -> 6.47 us
  waiting for transfers between devices: 54.5 us -> 0 us
  starting transfers between devices: 45.1 us -> 0 us
  Pallas kernels: 0 us -> 43.2 us
  other arithmetic: 33.8 us -> 0 us
    ppermute x12 -> x0, waiting for transfers between devices: 50 us -> none  [the longest x6 34 us: with_halo(): lax.ppermute(tail, axis, [(i, (i + 1) % count) for i in range(ends)])]
    pallas_call x0 -> x1, Pallas kernels: none -> 43.2 us  [per_device(): pl.pallas_call(level_kernel, out_shape=(jax.ShapeDtypeStruct((1, boxes, e...]
    ppermute x12 -> x0, starting transfers between devices: 38.4 us -> none  [the longest x6 30.5 us: with_halo(): lax.ppermute(tail, axis, [(i, (i + 1) % count) for i in range(ends)])]
    gather x38 -> x0, local copies, waits for them, and re-layouts: 26.5 us -> none  [the longest x36 22.9 us: ghost_planes(): chosen = jnp.take(tables[face_id], local_row, axis=0)]
    select_n x29 -> x0, other arithmetic: 20.4 us -> none  [the longest x21 12.2 us: ghost_planes(): results.append(jnp.where(is_valid, chosen, fallback))]
    slice x40 -> x0, local copies, waits for them, and re-layouts: 20 us -> none  [the longest x4 3.51 us: beside_cells(): low_shift = jnp.concatenate([zero_column, box_field[:, :, :-1]], axis=2)]
    reshape x15 -> x0, local copies, waits for them, and re-layouts: 17.6 us -> none  [the longest x6 8.54 us: beside_cells(): jnp.repeat(planes[5], box_edge, axis=2)]
    broadcast_in_dim x24 -> x0, local copies, waits for them, and re-layouts: 12.2 us -> none  [the longest x6 6.02 us: beside_cells(): jnp.repeat(planes[5], box_edge, axis=2)]
  transfers between devices with their start and end apart: 14 -> 0, of which waited for: 3 -> 0; matrix products, arithmetic and copies ran while one was open for 33% -> 0% of each run, Pallas kernels for 0% -> 0%
where the time goes in v1:
time: 50.5 us; the launch traced here: 50.3 us
  Pallas kernels  43.2 us (86%)
  local copies, waits for them, and re-layouts  6.47 us (13%)
  between operations  0.65 us (1%)
    pallas_call x1, Pallas kernels, per_device(): pl.pallas_call(level_kernel, out_shape=(jax.ShapeDtypeStruct((1, boxes, e...  43.2 us
    unnamed x13, local copies, waits for them, and re-layouts  6.47 us

profile of v1, /device:TPU:0, one launch (start us, length us, event | category | flops | bytes accessed | tf_op | source)
XLA Modules:
  0.0 50.3 jit_solution(11798619205614974361)
XLA Ops:
  0.6 0.0 copy-start
  0.6 1.4 %copy-done = f32[3,1,4,32,1024]{4,3,2,1,0:T(8,128)S(1)} copy-done((f32[3,1,4,32,1024]{4,3,2,1,0:T(8,128)S(1)}, f32[3,1,4,32,1024]{4,3,2,1,0:T(8,128)}, u32[]{:S(2)}) %copy-start) | copy-done | bytes 1572888
  2.0 0.0 copy-start.1
  2.0 0.9 %copy-done.1 = f32[1,2,8,16,256]{4,3,2,1,0:T(8,128)S(1)} copy-done((f32[1,2,8,16,256]{4,3,2,1,0:T(8,128)S(1)}, f32[1,2,8,16,256]{4,3,2,1,0:T(8,128)}, u32[]{:S(2)}) %copy-start.1) | copy-done | bytes 262168
  3.0 0.0 copy-start.2
  3.0 0.7 %copy-done.2 = s32[1,2,6]{2,1,0:T(2,128)S(1)} copy-done((s32[1,2,6]{2,1,0:T(2,128)S(1)}, s32[1,2,6]{2,1,0:T(2,128)}, u32[]{:S(2)}) %copy-start.2) | copy-done | bytes 72
  3.7 0.0 copy-start.3
  3.7 0.7 %copy-done.3 = s32[1,2,3]{2,1,0:T(2,128)S(1)} copy-done((s32[1,2,3]{2,1,0:T(2,128)S(1)}, s32[1,2,3]{2,1,0:T(2,128)}, u32[]{:S(2)}) %copy-start.3) | copy-done | bytes 48
  4.3 0.0 copy-start.4
  4.4 0.7 %copy-done.4 = s32[1,8]{1,0:T(1,128)S(1)} copy-done((s32[1,8]{1,0:T(1,128)S(1)}, s32[1,8]{1,0:T(1,128)}, u32[]{:S(2)}) %copy-start.4) | copy-done | bytes 56
  5.0 43.2 %shard_map.76 = (f32[1,2,32,1024]{3,2,1,0:T(8,128)S(1)}, f32[1,2,32,1024]{3,2,1,0:T(8,128)S(1)}, f32[16,16,256]{2,1,0:T(8,128)S(1)}) custom-call(f32[3,1,4,32,1024]{4,3,2,1,0:T(8,128)S(1)} %copy-done, s32[1,8]{1,0:T(1,128)S(1)} %copy-done.4, s32[1,2,6]{2,1,0:T(2,128)S(1)} %copy-done.2, s32[1,2,3]{2,1,0:T(2,128)S(1)} %copy-done.3, f32[16,16,256]{2,1,0:T(8,128)S(1)} %bitcast.2), custom_call_target="tpu_custom_call" | custom-call | tf_op jit(solution)/shard_map/pallas_call | solution.py:486
  48.2 0.7 %copy.11 = f32[1,2,32,1024]{3,2,1,0:T(8,128)} copy(f32[1,2,32,1024]{3,2,1,0:T(8,128)S(1)} %get-tuple-element.12) | data formatting | bytes 524288
  48.9 0.7 %copy.12 = f32[1,2,32,1024]{3,2,1,0:T(8,128)} copy(f32[1,2,32,1024]{3,2,1,0:T(8,128)S(1)} %get-tuple-element.13) | data formatting | bytes 524288
  49.6 0.7 %copy.13 = f32[1,2,8,16,256]{4,3,2,1,0:T(8,128)} copy(f32[1,2,8,16,256]{4,3,2,1,0:T(8,128)S(1)} %bitcast.3) | data formatting | bytes 524288
Async XLA Ops:
  0.6 1.4 %copy-start = (f32[3,1,4,32,1024]{4,3,2,1,0:T(8,128)S(1)}, f32[3,1,4,32,1024]{4,3,2,1,0:T(8,128)}, u32[]{:S(2)}) copy-start(f32[3,1,4,32,1024]{4,3,2,1,0:T(8,128)} %old_ref.1) | copy-start | bytes 4718596
  2.0 0.9 %copy-start.1 = (f32[1,2,8,16,256]{4,3,2,1,0:T(8,128)S(1)}, f32[1,2,8,16,256]{4,3,2,1,0:T(8,128)}, u32[]{:S(2)}) copy-start(f32[1,2,8,16,256]{4,3,2,1,0:T(8,128)} %param.9) | copy-start | bytes 786436
  3.0 0.7 %copy-start.2 = (s32[1,2,6]{2,1,0:T(2,128)S(1)}, s32[1,2,6]{2,1,0:T(2,128)}, u32[]{:S(2)}) copy-start(s32[1,2,6]{2,1,0:T(2,128)} %link_ref.1) | copy-start | bytes 148
  3.7 0.7 %copy-start.3 = (s32[1,2,3]{2,1,0:T(2,128)S(1)}, s32[1,2,3]{2,1,0:T(2,128)}, u32[]{:S(2)}) copy-start(s32[1,2,3]{2,1,0:T(2,128)} %parent_ref.1) | copy-start | bytes 76
  4.3 0.7 %copy-start.4 = (s32[1,8]{1,0:T(1,128)S(1)}, s32[1,8]{1,0:T(1,128)}, u32[]{:S(2)}) copy-start(s32[1,8]{1,0:T(1,128)} %count_ref.1) | copy-start | bytes 100

commit v2 on v1

--- a/solution.py
+++ b/solution.py
@@ -11,25 +11,33 @@
 TILE = 8
 PAD = 8
 FACES = 6
+VMEM_BYTES = 60 * 1024 * 1024
 
 
 def level_kernel(
     old_ref,
-    count_ref,
-    link_ref,
-    parent_ref,
+    count_hbm,
+    link_hbm,
+    parent_hbm,
     coarse_ref,
     smooth_out,
     residual_out,
     coarse_out,
+    count_ref,
+    link_ref,
+    parent_ref,
     held_sol,
     held_rhs,
     held_coef,
-    send_right,
+    coef_out,
+    coef_in,
+    half_out,
+    half_in,
     sol,
     coef,
     weights,
     diagonal,
+    inverse,
     scaled_rhs,
     plane_out,
     res_rows,
@@ -66,15 +74,15 @@
     held = (held_sol, held_rhs, held_coef)
 
     def load(field):
-        return pltpu.make_async_copy(
-            old_ref.at[field, 0], held[field].at[pl.ds(0, slots)], load_sem.at[field]
+        return pltpu.make_async_copy(old_ref.at[field, 0], held[field], load_sem.at[field])
+
+    coarse_load = pltpu.make_async_copy(coarse_ref, coarse_buf, load_sem.at[3])
+    tables = [
+        pltpu.make_async_copy(source, target, load_sem.at[4 + i])
+        for i, (source, target) in enumerate(
+            ((count_hbm, count_ref), (link_hbm, link_ref), (parent_hbm, parent_ref))
         )
-
-    coarse_load = pltpu.make_async_copy(coarse_ref, coarse_buf, load_sem.at[3])
-    for field in (2, 0, 1):
-        load(field).start()
-    coarse_load.start()
-
+    ]
     barrier = pltpu.get_barrier_semaphore()
 
     @pl.when(has_left)
@@ -92,30 +100,58 @@
             device_id=(place, lax.rem(group + step, groups)),
             device_id_type=MESH,
         )
-    pl.semaphore_wait(
-        barrier, groups - 1 + has_left.astype(jnp.int32) + has_right.astype(jnp.int32)
-    )
-
-    def move_left(field):
-        return pltpu.make_async_remote_copy(
-            src_ref=old_ref.at[field, 0, 0],
-            dst_ref=held[field].at[slots + 1],
-            send_sem=move_send.at[0, field],
-            recv_sem=move_recv.at[0, field],
-            device_id=(place - 1, group),
-            device_id_type=MESH,
-        )
-
-    def move_right(field):
-        return pltpu.make_async_remote_copy(
-            src_ref=send_right.at[field],
-            dst_ref=held[field].at[slots],
-            send_sem=move_send.at[1, field],
-            recv_sem=move_recv.at[1, field],
-            device_id=(place + 1, group),
-            device_id_type=MESH,
-        )
-
+    for table in tables:
+        table.start()
+    for field in (2, 0, 1):
+        load(field).start()
+    coarse_load.start()
+
+    shape = (columns, TILE, LANES)
+    lane = lax.broadcasted_iota(jnp.int32, shape, 2)
+    column = lax.broadcasted_iota(jnp.int32, shape, 0)
+    depth = lane & (edge - 1)
+    low_depth = depth == 0
+    high_depth = depth == edge - 1
+    low_lane = lane < edge
+    high_lane = lane >= LANES - edge
+    low_row = low_lane & (column == 0)
+    high_row = high_lane & (column == columns - 1)
+    edge_masks = (None, None, low_row, high_row, low_depth, high_depth)
+    parity = (
+        lax.broadcasted_iota(jnp.int32, shape, 1)
+        + column * (LANES // edge)
+        + (lane >> (edge.bit_length() - 1))
+        + depth
+    ) & 1
+    pairs = columns // 2
+    even_line = ((lane[:pairs] >> (edge.bit_length() - 1)) & 1) == 0
+    odd_cell = parity[:pairs] == 1
+
+    def spread(rows):
+        return jnp.stack([rows[:, c * LANES : (c + 1) * LANES] for c in range(columns)])
+
+    def flatten(block):
+        return jnp.concatenate([block[c] for c in range(columns)], axis=1)
+
+    def thin(block, colour):
+        low, high = block[:pairs], block[pairs:]
+        low_next = pltpu.roll(low, LANES - edge, 2)
+        high_next = pltpu.roll(high, edge, 2)
+        if colour:
+            low = jnp.where(odd_cell, low, low_next)
+            high = jnp.where(odd_cell, high, high_next)
+        else:
+            low = jnp.where(odd_cell, low_next, low)
+            high = jnp.where(odd_cell, high_next, high)
+        return jnp.where(even_line, low, high)
+
+    def thicken(block):
+        low = jnp.where(even_line, block, pltpu.roll(block, edge, 2))
+        high = jnp.where(even_line, pltpu.roll(block, LANES - edge, 2), block)
+        return jnp.concatenate([low, high], axis=0)
+
+    for table in tables:
+        table.wait()
     start = jnp.int32(0)
     for other in range(curve):
         start = start + jnp.where(other < place, count_ref[0, other], 0)
@@ -124,38 +160,70 @@
         end = end + jnp.where(other == place, count_ref[0, other], 0)
     first = place * boxes
     right_slot = jnp.clip(first + boxes - start, 0, slots - 1)
-    own_rows = []
-    for b in range(boxes):
-        wanted = first + b
-        own = jnp.clip(wanted - start, 0, slots - 1)
-        own_rows.append(
-            jnp.where(wanted < start, slots, jnp.where(wanted >= end, slots + 1, own))
+    own_slots = [jnp.clip(first + b - start, 0, slots - 1) for b in range(boxes)]
+    load(2).wait()
+    for side, slot in ((0, 0), (1, right_slot)):
+        coef_out[side] = held_coef[slot]
+    pl.semaphore_wait(
+        barrier, groups - 1 + has_left.astype(jnp.int32) + has_right.astype(jnp.int32)
+    )
+
+    def move(side, part):
+        if part == 0:
+            source, target = coef_out.at[side], coef_in.at[side]
+        else:
+            source, target = half_out.at[part - 1, side], half_in.at[part - 1, side]
+        return pltpu.make_async_remote_copy(
+            src_ref=source,
+            dst_ref=target,
+            send_sem=move_send.at[side, part],
+            recv_sem=move_recv.at[side, part],
+            device_id=(place + 2 * side - 1, group),
+            device_id_type=MESH,
         )
 
-    for field in (2, 0, 1):
-
+    def move_start(part):
         @pl.when(has_left)
-        def _(field=field):
-            move_left(field).start()
-
-        load(field).wait()
-        chosen = held[field][0]
-        for s in range(1, slots):
-            chosen = jnp.where(right_slot == s, held[field][s], chosen)
-        send_right[field] = chosen
+        def _():
+            move(0, part).start()
 
         @pl.when(has_right)
-        def _(field=field):
-            move_right(field).start()
-
-    def move_wait(field):
+        def _():
+            move(1, part).start()
+
+    def thin_out(part, field, colour):
+        for side, slot in ((0, 0), (1, right_slot)):
+            for t in range(tiles):
+                rows = slice(t * TILE, (t + 1) * TILE)
+                half_out[part - 1, side, :, rows, :] = thin(
+                    spread(held[field][slot, rows, :]), colour
+                )
+        move_start(part)
+
+    move_start(0)
+    load(0).wait()
+    thin_out(1, 0, 1)
+    load(1).wait()
+    thin_out(2, 1, 0)
+    thin_out(3, 1, 1)
+
+    def move_wait(part):
         @pl.when(has_right)
         def _():
-            move_left(field).wait_recv()
+            move(0, part).wait_recv()
 
         @pl.when(has_left)
         def _():
-            move_right(field).wait_recv()
+            move(1, part).wait_recv()
+
+    def moved(field, b, t, arrived):
+        rows = slice(t * TILE, (t + 1) * TILE)
+        block = spread(held[field][own_slots[b], rows, :])
+        if b == 0:
+            block = jnp.where(first + b < start, arrived(1, rows), block)
+        if b == boxes - 1:
+            block = jnp.where(first + b >= end, arrived(0, rows), block)
+        return block
 
     def face_to(k, side):
         return pltpu.make_async_remote_copy(
@@ -210,24 +278,6 @@
                         plane,
                     )
                 ref[b, :, row : row + 1, :] = plane
-
-    shape = (columns, TILE, LANES)
-    lane = lax.broadcasted_iota(jnp.int32, shape, 2)
-    column = lax.broadcasted_iota(jnp.int32, shape, 0)
-    depth = lane & (edge - 1)
-    low_depth = depth == 0
-    high_depth = depth == edge - 1
-    low_lane = lane < edge
-    high_lane = lane >= LANES - edge
-    low_row = low_lane & (column == 0)
-    high_row = high_lane & (column == columns - 1)
-    edge_masks = (None, None, low_row, high_row, low_depth, high_depth)
-    parity = (
-        lax.broadcasted_iota(jnp.int32, shape, 1)
-        + column * (LANES // edge)
-        + (lane >> (edge.bit_length() - 1))
-        + depth
-    ) & 1
 
     def around(ref, b, t):
         rows = slice(PAD + t * TILE, PAD + (t + 1) * TILE)
@@ -255,12 +305,6 @@
             ),
         )
 
-    def spread(rows):
-        return jnp.stack([rows[:, c * LANES : (c + 1) * LANES] for c in range(columns)])
-
-    def flatten(block):
-        return jnp.concatenate([block[c] for c in range(columns)], axis=1)
-
     target = lax.broadcasted_iota(jnp.int32, merge_map.shape, 0)
     target = ((target >> edge.bit_length()) * half) + (
         (target & (edge - 1)) >> 1
@@ -274,18 +318,19 @@
         ).astype(jnp.float32)
         pack[b, half : half + TILE, :] = jnp.full((TILE, half * half), label, jnp.float32)
 
-    def take(field, ref):
-        for b in range(boxes):
-            for t in range(tiles):
-                ref[b, :, PAD + t * TILE : PAD + (t + 1) * TILE, :] = spread(
-                    held[field][own_rows[b], t * TILE : (t + 1) * TILE, :]
-                )
-
-    move_wait(2)
-    take(2, coef)
+    move_wait(0)
+    for b in range(boxes):
+        for t in range(tiles):
+            coef[b, :, PAD + t * TILE : PAD + (t + 1) * TILE, :] = moved(
+                2, b, t, lambda side, rows: spread(coef_in[side, rows, :])
+            )
     faces_start(0, coef)
-    move_wait(0)
-    take(0, sol)
+    move_wait(1)
+    for b in range(boxes):
+        for t in range(tiles):
+            sol[b, :, PAD + t * TILE : PAD + (t + 1) * TILE, :] = moved(
+                0, b, t, lambda side, rows: thicken(half_in[0, side, :, rows, :])
+            )
     faces_start(1, sol)
     faces_wait(0)
     ghost_rows(0, coef, True)
@@ -306,18 +351,17 @@
                 if f >= 2:
                     weight = jnp.where(edge_masks[f], weight * linked[b][f], weight)
                 kept.append(weight)
-            inverse = 1.0 / total
+            over = 1.0 / total
             diagonal[b, t] = total
-            scaled_rhs[b, t] = inverse
+            inverse[b, t] = over
             for f in range(FACES):
-                weights[b, t, f] = kept[f] * inverse
-
-    move_wait(1)
-    for b in range(boxes):
-        for t in range(tiles):
-            scaled_rhs[b, t] = scaled_rhs[b, t] * spread(
-                held[1][own_rows[b], t * TILE : (t + 1) * TILE, :]
-            )
+                weights[b, t, f] = kept[f] * over
+
+    def scale_rhs(part, arrived):
+        move_wait(part)
+        for b in range(boxes):
+            for t in range(tiles):
+                scaled_rhs[b, t] = inverse[b, t] * moved(1, b, t, arrived)
 
     def relaxed(b, t):
         here, near = around(sol, b, t)
@@ -337,7 +381,17 @@
                     parity == colour, total, here
                 )
 
+    scale_rhs(2, lambda side, rows: thicken(half_in[1, side, :, rows, :]))
     for step in range(4):
+        if step == 1:
+            scale_rhs(
+                3,
+                lambda side, rows: jnp.where(
+                    parity == 0,
+                    thicken(half_in[1, side, :, rows, :]),
+                    thicken(half_in[2, side, :, rows, :]),
+                ),
+            )
         sweep(step % 2, inner)
         faces_wait(step + 1)
         ghost_rows(step + 1, sol, False)
@@ -426,15 +480,15 @@
 
     @pl.when(has_left)
     def _():
-        for field in range(3):
-            move_left(field).wait_send()
+        for part in range(4):
+            move(0, part).wait_send()
         for k in range(6):
             face_to(k, 0).wait_send()
 
     @pl.when(has_right)
     def _():
-        for field in range(3):
-            move_right(field).wait_send()
+        for part in range(4):
+            move(1, part).wait_send()
         for k in range(6):
             face_to(k, 1).wait_send()
 
@@ -443,8 +497,17 @@
     coarse_store.wait()
 
 
+def hand_out_kernel(*refs):
+    sems = refs[6]
+    copies = [pltpu.make_async_copy(refs[i], refs[3 + i], sems.at[i]) for i in range(3)]
+    for copy in copies:
+        copy.start()
+    for copy in copies:
+        copy.wait()
+
+
 def per_device(old_fields, old_count, neighbours, parents, coarse_source):
-    fields, _, slots, edge, cells = old_fields.shape
+    _, _, slots, edge, cells = old_fields.shape
     boxes = neighbours.shape[1]
     groups = lax.axis_size("grp")
     _, coarse_boxes, octants, half, quarter = coarse_source.shape
@@ -454,13 +517,20 @@
     f32 = jnp.float32
     coarse_slots = coarse_boxes * octants
     scratch = [
-        pltpu.VMEM((slots + 2, edge, cells), f32),
-        pltpu.VMEM((slots + 2, edge, cells), f32),
-        pltpu.VMEM((slots + 2, edge, cells), f32),
-        pltpu.VMEM((fields, edge, cells), f32),
+        pltpu.SMEM(old_count.shape, jnp.int32),
+        pltpu.SMEM(neighbours.shape, jnp.int32),
+        pltpu.SMEM(parents.shape, jnp.int32),
+        pltpu.VMEM((slots, edge, cells), f32),
+        pltpu.VMEM((slots, edge, cells), f32),
+        pltpu.VMEM((slots, edge, cells), f32),
+        pltpu.VMEM((2, edge, cells), f32),
+        pltpu.VMEM((2, edge, cells), f32),
+        pltpu.VMEM((3, 2, columns // 2, edge, LANES), f32),
+        pltpu.VMEM((3, 2, columns // 2, edge, LANES), f32),
         pltpu.VMEM((boxes, columns, padded, LANES), f32),
         pltpu.VMEM((boxes, columns, padded, LANES), f32),
         pltpu.VMEM((boxes, tiles, FACES, columns, TILE, LANES), f32),
+        pltpu.VMEM((boxes, tiles, columns, TILE, LANES), f32),
         pltpu.VMEM((boxes, tiles, columns, TILE, LANES), f32),
         pltpu.VMEM((boxes, tiles, columns, TILE, LANES), f32),
         pltpu.VMEM((boxes, edge, cells), f32),
@@ -472,9 +542,9 @@
         pltpu.VMEM((coarse_slots, half, quarter), f32),
         pltpu.VMEM((6, 2, boxes, columns, 1, LANES), f32),
         pltpu.VMEM((6, 2, boxes, columns, 1, LANES), f32),
-        pltpu.SemaphoreType.DMA((4,)),
-        pltpu.SemaphoreType.DMA((2, 3)),
-        pltpu.SemaphoreType.DMA((2, 3)),
+        pltpu.SemaphoreType.DMA((7,)),
+        pltpu.SemaphoreType.DMA((2, 4)),
+        pltpu.SemaphoreType.DMA((2, 4)),
         pltpu.SemaphoreType.DMA((6, 2)),
         pltpu.SemaphoreType.DMA((6, 2)),
         pltpu.SemaphoreType.DMA((groups - 1,)),
@@ -482,7 +552,7 @@
         pltpu.SemaphoreType.DMA((3,)),
     ]
     anywhere = pl.BlockSpec(memory_space=pl.ANY)
-    scalars = pl.BlockSpec(memory_space=pltpu.SMEM)
+    in_hbm = pl.BlockSpec(memory_space=pltpu.HBM)
     smoothed, residual, coarse_rhs = pl.pallas_call(
         level_kernel,
         out_shape=(
@@ -490,11 +560,11 @@
             jax.ShapeDtypeStruct((1, boxes, edge, cells), f32),
             jax.ShapeDtypeStruct((coarse_slots, half, quarter), f32),
         ),
-        in_specs=[anywhere, scalars, scalars, scalars, anywhere],
+        in_specs=[in_hbm] * 5,
         out_specs=(anywhere, anywhere, anywhere),
         scratch_shapes=scratch,
         compiler_params=pltpu.CompilerParams(
-            collective_id=0, has_side_effects=True, vmem_limit_bytes=48 * 1024 * 1024
+            collective_id=0, has_side_effects=True, vmem_limit_bytes=VMEM_BYTES
         ),
     )(
         old_fields,
@@ -503,6 +573,15 @@
         parents,
         coarse_source.reshape(coarse_slots, half, quarter),
     )
+    results = (smoothed, residual, coarse_rhs)
+    smoothed, residual, coarse_rhs = pl.pallas_call(
+        hand_out_kernel,
+        out_shape=tuple(jax.ShapeDtypeStruct(part.shape, f32) for part in results),
+        in_specs=[anywhere] * 3,
+        out_specs=(in_hbm,) * 3,
+        scratch_shapes=[pltpu.SemaphoreType.DMA((3,))],
+        compiler_params=pltpu.CompilerParams(vmem_limit_bytes=VMEM_BYTES),
+    )(*results)
     return smoothed, residual, coarse_rhs.reshape(coarse_source.shape)
 
 

time: 50.5 us -> 65.9 us (1.30)
  Pallas kernels: 43.2 us -> 65.1 us
  local copies, waits for them, and re-layouts: 6.47 us -> 0 us
    pallas_call x0 -> x1, Pallas kernels: none -> 25 us  [per_device(): pl.pallas_call(hand_out_kernel, out_shape=tuple((jax.ShapeDtypeStruct(par...]
    unnamed x13 -> x0, local copies, waits for them, and re-layouts: 6.47 us -> none
    pallas_call x1, Pallas kernels: 43.2 us -> 40.2 us  [per_device(): pl.pallas_call(level_kernel, out_shape=(jax.ShapeDtypeStruct((1, boxes, e...]
where the time goes in v2:
time: 65.9 us; the launch traced here: 65.8 us
  Pallas kernels  65.1 us (99%)
    pallas_call x1, Pallas kernels, per_device(): pl.pallas_call(level_kernel, out_shape=(jax.ShapeDtypeStruct((1, boxes, e...  40.2 us
    pallas_call x1, Pallas kernels, per_device(): pl.pallas_call(hand_out_kernel, out_shape=tuple((jax.ShapeDtypeStruct(par...  25 us

profile of v2, /device:TPU:0, one launch (start us, length us, event | category | flops | bytes accessed | tf_op | source)
XLA Modules:
  0.0 65.8 jit_solution(2955110041453371967)
XLA Ops:
  0.6 40.2 %shard_map.76 = (f32[1,2,32,1024]{3,2,1,0:T(8,128)}, f32[1,2,32,1024]{3,2,1,0:T(8,128)}, f32[16,16,256]{2,1,0:T(8,128)}) custom-call(f32[3,1,4,32,1024]{4,3,2,1,0:T(8,128)} %old_ref.1, s32[1,8]{1,0:T(1,128)} %count_hbm.1, s32[1,2,6]{2,1,0:T(2,128)} %link_hbm.1, s32[1,2,3]{2,1,0:T(2,128)} %parent_hbm.1, f32[16,16,256]{2,1,0:T(8,128)} %bitcast.2), custom_call_target="tpu_custom_call" | custom-call | tf_op jit(solution)/shard_map/pallas_call | solution.py:556
  40.8 25.0 %shard_map.77 = (f32[1,2,32,1024]{3,2,1,0:T(8,128)}, f32[1,2,32,1024]{3,2,1,0:T(8,128)}, f32[16,16,256]{2,1,0:T(8,128)}) custom-call(f32[1,2,32,1024]{3,2,1,0:T(8,128)} %get-tuple-element.9.refs_0_, f32[1,2,32,1024]{3,2,1,0:T(8,128)} %get-tuple-element.10.refs_1_, f32[16,16,256]{2,1,0:T(8,128)} %get-tuple-element.11.refs_2_), custom_call_target="tpu_custom_call" | custom-call | tf_op jit(solution)/shard_map/pallas_call | solution.py:577

commit v3 on v2

--- a/solution.py
+++ b/solution.py
@@ -1,3 +1,5 @@
+import functools
+
 import jax
 import jax.numpy as jnp
 from jax import lax
@@ -15,14 +17,14 @@
 
 
 def level_kernel(
+    coarse_slots,
     old_ref,
     count_hbm,
     link_hbm,
     parent_hbm,
-    coarse_ref,
     smooth_out,
     residual_out,
-    coarse_out,
+    packs_out,
     count_ref,
     link_ref,
     parent_ref,
@@ -44,8 +46,6 @@
     merge_map,
     merged,
     pack,
-    got_pack,
-    coarse_buf,
     face_out,
     face_in,
     load_sem,
@@ -68,7 +68,6 @@
     tiles = edge // TILE
     columns = cells // LANES
     half = edge // 2
-    coarse_slots = coarse_buf.shape[0]
     has_left = place > 0
     has_right = place < curve - 1
     held = (held_sol, held_rhs, held_coef)
@@ -76,9 +75,8 @@
     def load(field):
         return pltpu.make_async_copy(old_ref.at[field, 0], held[field], load_sem.at[field])
 
-    coarse_load = pltpu.make_async_copy(coarse_ref, coarse_buf, load_sem.at[3])
     tables = [
-        pltpu.make_async_copy(source, target, load_sem.at[4 + i])
+        pltpu.make_async_copy(source, target, load_sem.at[3 + i])
         for i, (source, target) in enumerate(
             ((count_hbm, count_ref), (link_hbm, link_ref), (parent_hbm, parent_ref))
         )
@@ -104,7 +102,6 @@
         table.start()
     for field in (2, 0, 1):
         load(field).start()
-    coarse_load.start()
 
     shape = (columns, TILE, LANES)
     lane = lax.broadcasted_iota(jnp.int32, shape, 2)
@@ -123,6 +120,13 @@
         + (lane >> (edge.bit_length() - 1))
         + depth
     ) & 1
+    plane_shape = (columns, 1, LANES)
+    plane_lane = lax.broadcasted_iota(jnp.int32, plane_shape, 2)
+    plane_parity = (
+        lax.broadcasted_iota(jnp.int32, plane_shape, 0) * (LANES // edge)
+        + (plane_lane >> (edge.bit_length() - 1))
+        + (plane_lane & (edge - 1))
+    ) & 1
     pairs = columns // 2
     even_line = ((lane[:pairs] >> (edge.bit_length() - 1)) & 1) == 0
     odd_cell = parity[:pairs] == 1
@@ -235,10 +239,10 @@
             device_id_type=MESH,
         )
 
-    def faces_start(k, ref):
+    def faces_start(k, plane_of):
         for b in range(boxes):
-            face_out[k, 0, b] = ref[b, :, PAD : PAD + 1, :]
-            face_out[k, 1, b] = ref[b, :, PAD + edge - 1 : PAD + edge, :]
+            for side in range(2):
+                face_out[k, side, b] = plane_of(b, side)
 
         @pl.when(has_left)
         def _():
@@ -256,28 +260,45 @@
         @pl.when(has_right)
         def _():
             face_to(k, 0).wait_recv()
+
+    def own_planes(ref):
+        return lambda b, side: ref[
+            b, :, PAD + side * (edge - 1) : PAD + side * (edge - 1) + 1, :
+        ]
 
     links = [[link_ref[0, b, f] for f in range(FACES)] for b in range(boxes)]
     linked = [[jnp.where(t >= 0, 1.0, 0.0) for t in row] for row in links]
     beside = [[jnp.clip(t - first, 0, boxes - 1) for t in row] for row in links]
 
+    def arrived_plane(k, b, f, plane):
+        base = first + (2 * f - 1) * boxes
+        for other in range(boxes):
+            plane = jnp.where(
+                (links[b][f] >= 0) & (links[b][f] == base + other),
+                face_in[k, 1 - f, other],
+                plane,
+            )
+        return plane
+
+    no_plane = jnp.zeros((columns, 1, LANES), jnp.float32)
+    ghost_at = (PAD - 1, PAD + edge)
+
     def ghost_rows(k, ref, keep_own):
         for b in range(boxes):
-            for f, side, base, row, own in (
-                (0, 1, first - boxes, PAD - 1, PAD),
-                (1, 0, first + boxes, PAD + edge, PAD + edge - 1),
-            ):
-                if keep_own:
-                    plane = ref[b, :, own : own + 1, :]
-                else:
-                    plane = jnp.zeros((columns, 1, LANES), jnp.float32)
-                for other in range(boxes):
-                    plane = jnp.where(
-                        (links[b][f] >= 0) & (links[b][f] == base + other),
-                        face_in[k, side, other],
-                        plane,
-                    )
-                ref[b, :, row : row + 1, :] = plane
+            for f in range(2):
+                plane = own_planes(ref)(b, f) if keep_own else no_plane
+                ref[b, :, ghost_at[f] : ghost_at[f] + 1, :] = arrived_plane(k, b, f, plane)
+
+    def advance_ghosts(colour):
+        for b in range(boxes):
+            for f in range(2):
+                row = slice(ghost_at[f], ghost_at[f] + 1)
+                plane = sol[b, :, row, :]
+                sol[b, :, row, :] = jnp.where(
+                    ((plane_parity + 1 - f) & 1) == colour,
+                    plane + arrived_plane(2, b, f, no_plane) * own_planes(sol)(b, f),
+                    plane,
+                )
 
     def around(ref, b, t):
         rows = slice(PAD + t * TILE, PAD + (t + 1) * TILE)
@@ -324,14 +345,14 @@
             coef[b, :, PAD + t * TILE : PAD + (t + 1) * TILE, :] = moved(
                 2, b, t, lambda side, rows: spread(coef_in[side, rows, :])
             )
-    faces_start(0, coef)
+    faces_start(0, own_planes(coef))
     move_wait(1)
     for b in range(boxes):
         for t in range(tiles):
             sol[b, :, PAD + t * TILE : PAD + (t + 1) * TILE, :] = moved(
                 0, b, t, lambda side, rows: thicken(half_in[0, side, :, rows, :])
             )
-    faces_start(1, sol)
+    faces_start(1, own_planes(sol))
     faces_wait(0)
     ghost_rows(0, coef, True)
     for b in range(boxes):
@@ -357,6 +378,13 @@
             for f in range(FACES):
                 weights[b, t, f] = kept[f] * over
 
+    faces_start(
+        2,
+        lambda b, side: weights[
+            b, side * (tiles - 1), side, :, side * (TILE - 1) : side * (TILE - 1) + 1, :
+        ],
+    )
+
     def scale_rhs(part, arrived):
         move_wait(part)
         for b in range(boxes):
@@ -382,21 +410,46 @@
                 )
 
     scale_rhs(2, lambda side, rows: thicken(half_in[1, side, :, rows, :]))
-    for step in range(4):
-        if step == 1:
-            scale_rhs(
-                3,
-                lambda side, rows: jnp.where(
-                    parity == 0,
-                    thicken(half_in[1, side, :, rows, :]),
-                    thicken(half_in[2, side, :, rows, :]),
-                ),
-            )
-        sweep(step % 2, inner)
-        faces_wait(step + 1)
-        ghost_rows(step + 1, sol, False)
-        sweep(step % 2, outer)
-        faces_start(step + 2, sol)
+    def next_planes(colour):
+        def plane_of(b, side):
+            t = side * (tiles - 1)
+            here, near = around(sol, b, t)
+            total = scaled_rhs[b, t]
+            for f in range(FACES):
+                if f != side:
+                    total = total + weights[b, t, f] * near[f]
+            block = jnp.where(parity == colour, total, here)
+            return block[:, side * (TILE - 1) : side * (TILE - 1) + 1, :]
+
+        return plane_of
+
+    sweep(0, inner)
+    faces_wait(1)
+    ghost_rows(1, sol, False)
+    sweep(0, outer)
+    scale_rhs(
+        3,
+        lambda side, rows: jnp.where(
+            parity == 0,
+            thicken(half_in[1, side, :, rows, :]),
+            thicken(half_in[2, side, :, rows, :]),
+        ),
+    )
+    faces_start(3, next_planes(1))
+    sweep(1, inner)
+    faces_wait(2)
+    faces_wait(3)
+    ghost_rows(3, sol, False)
+    sweep(1, outer)
+    advance_ghosts(1)
+    sweep(0, outer)
+    faces_start(4, next_planes(1))
+    sweep(0, inner)
+    sweep(1, inner)
+    faces_wait(4)
+    ghost_rows(4, sol, False)
+    sweep(1, outer)
+    advance_ghosts(1)
 
     for b in range(boxes):
         for t in range(tiles):
@@ -414,10 +467,7 @@
                     diagonal[b, t] * (total - here)
                 )
 
-    leave(inner)
-    faces_wait(5)
-    ghost_rows(5, sol, False)
-    leave(outer)
+    leave(range(tiles))
     residual_store = pltpu.make_async_copy(res_rows, residual_out.at[0], store_sem.at[1])
     residual_store.start()
 
@@ -443,7 +493,7 @@
     def pack_to(step):
         return pltpu.make_async_remote_copy(
             src_ref=pack,
-            dst_ref=got_pack.at[step - 1],
+            dst_ref=packs_out.at[step],
             send_sem=pack_send.at[step - 1],
             recv_sem=pack_recv.at[step - 1],
             device_id=(place, lax.rem(group + step, groups)),
@@ -452,28 +502,10 @@
 
     for step in range(1, groups):
         pack_to(step).start()
-    coarse_load.wait()
-
-    def place_from(refs):
-        for ref in refs:
-            for b in range(boxes):
-                label = ref[b, half : half + TILE, :]
-                label = jnp.concatenate([label] * (half // TILE), axis=0)
-                values = ref[b, 0:half, :]
-
-                def put(s, carry, label=label, values=values):
-                    mine = (group * coarse_slots + s).astype(jnp.float32)
-                    coarse_buf[s] = jnp.where(label == mine, values, coarse_buf[s])
-                    return carry
-
-                lax.fori_loop(0, coarse_slots, put, 0, unroll=True)
-
-    place_from([pack])
+    own_store = pltpu.make_async_copy(pack, packs_out.at[0], store_sem.at[2])
+    own_store.start()
     for step in range(1, groups):
         pack_to(step).wait_recv()
-        place_from([got_pack.at[step - 1]])
-    coarse_store = pltpu.make_async_copy(coarse_buf, coarse_out, store_sem.at[2])
-    coarse_store.start()
 
     for step in range(1, groups):
         pack_to(step).wait_send()
@@ -482,28 +514,73 @@
     def _():
         for part in range(4):
             move(0, part).wait_send()
-        for k in range(6):
+        for k in range(5):
             face_to(k, 0).wait_send()
 
     @pl.when(has_right)
     def _():
         for part in range(4):
             move(1, part).wait_send()
-        for k in range(6):
+        for k in range(5):
             face_to(k, 1).wait_send()
 
     smooth_store.wait()
     residual_store.wait()
-    coarse_store.wait()
-
-
-def hand_out_kernel(*refs):
-    sems = refs[6]
-    copies = [pltpu.make_async_copy(refs[i], refs[3 + i], sems.at[i]) for i in range(3)]
-    for copy in copies:
-        copy.start()
-    for copy in copies:
-        copy.wait()
+    own_store.wait()
+
+
+def hand_out_kernel(
+    smooth_in,
+    residual_in,
+    packs_in,
+    coarse_in,
+    smooth_out,
+    residual_out,
+    coarse_out,
+    smooth_buf,
+    residual_buf,
+    packs,
+    coarse,
+    load_sem,
+    store_sem,
+):
+    group = lax.axis_index("grp")
+    groups, boxes = packs.shape[:2]
+    slots, half = coarse.shape[:2]
+    loads = [
+        pltpu.make_async_copy(source, target, load_sem.at[i])
+        for i, (source, target) in enumerate(
+            (
+                (packs_in, packs),
+                (coarse_in, coarse),
+                (smooth_in, smooth_buf),
+                (residual_in, residual_buf),
+            )
+        )
+    ]
+    stores = [
+        pltpu.make_async_copy(source, target, store_sem.at[i])
+        for i, (source, target) in enumerate(
+            ((smooth_buf, smooth_out), (residual_buf, residual_out), (coarse, coarse_out))
+        )
+    ]
+    for load in loads:
+        load.start()
+    for load in loads:
+        load.wait()
+    stores[0].start()
+    stores[1].start()
+    for source in range(groups):
+        for b in range(boxes):
+            label = packs[source, b, half : half + TILE, :]
+            label = jnp.concatenate([label] * (half // TILE), axis=0)
+            values = packs[source, b, 0:half, :]
+            for s in range(slots):
+                mine = (group * slots + s).astype(jnp.float32)
+                coarse[s] = jnp.where(label == mine, values, coarse[s])
+    stores[2].start()
+    for store in stores:
+        store.wait()
 
 
 def per_device(old_fields, old_count, neighbours, parents, coarse_source):
@@ -538,29 +615,27 @@
         pltpu.VMEM((cells, quarter), jnp.bfloat16),
         pltpu.VMEM((boxes, quarter // LANES, edge, LANES), f32),
         pltpu.VMEM((boxes, half + TILE, quarter), f32),
-        pltpu.VMEM((groups - 1, boxes, half + TILE, quarter), f32),
-        pltpu.VMEM((coarse_slots, half, quarter), f32),
-        pltpu.VMEM((6, 2, boxes, columns, 1, LANES), f32),
-        pltpu.VMEM((6, 2, boxes, columns, 1, LANES), f32),
-        pltpu.SemaphoreType.DMA((7,)),
+        pltpu.VMEM((5, 2, boxes, columns, 1, LANES), f32),
+        pltpu.VMEM((5, 2, boxes, columns, 1, LANES), f32),
+        pltpu.SemaphoreType.DMA((6,)),
         pltpu.SemaphoreType.DMA((2, 4)),
         pltpu.SemaphoreType.DMA((2, 4)),
-        pltpu.SemaphoreType.DMA((6, 2)),
-        pltpu.SemaphoreType.DMA((6, 2)),
+        pltpu.SemaphoreType.DMA((5, 2)),
+        pltpu.SemaphoreType.DMA((5, 2)),
         pltpu.SemaphoreType.DMA((groups - 1,)),
         pltpu.SemaphoreType.DMA((groups - 1,)),
         pltpu.SemaphoreType.DMA((3,)),
     ]
     anywhere = pl.BlockSpec(memory_space=pl.ANY)
     in_hbm = pl.BlockSpec(memory_space=pltpu.HBM)
-    smoothed, residual, coarse_rhs = pl.pallas_call(
-        level_kernel,
+    smoothed, residual, packs = pl.pallas_call(
+        functools.partial(level_kernel, coarse_slots),
         out_shape=(
             jax.ShapeDtypeStruct((1, boxes, edge, cells), f32),
             jax.ShapeDtypeStruct((1, boxes, edge, cells), f32),
-            jax.ShapeDtypeStruct((coarse_slots, half, quarter), f32),
+            jax.ShapeDtypeStruct((groups, boxes, half + TILE, quarter), f32),
         ),
-        in_specs=[in_hbm] * 5,
+        in_specs=[in_hbm] * 4,
         out_specs=(anywhere, anywhere, anywhere),
         scratch_shapes=scratch,
         compiler_params=pltpu.CompilerParams(
@@ -571,17 +646,19 @@
         old_count,
         neighbours,
         parents,
-        coarse_source.reshape(coarse_slots, half, quarter),
-    )
-    results = (smoothed, residual, coarse_rhs)
+    )
+    coarse = coarse_source.reshape(coarse_slots, half, quarter)
+    parts = (smoothed, residual, packs, coarse)
+    results = (smoothed, residual, coarse)
     smoothed, residual, coarse_rhs = pl.pallas_call(
         hand_out_kernel,
         out_shape=tuple(jax.ShapeDtypeStruct(part.shape, f32) for part in results),
-        in_specs=[anywhere] * 3,
+        in_specs=[in_hbm] * 4,
         out_specs=(in_hbm,) * 3,
-        scratch_shapes=[pltpu.SemaphoreType.DMA((3,))],
+        scratch_shapes=[pltpu.VMEM(part.shape, f32) for part in parts]
+        + [pltpu.SemaphoreType.DMA((4,)), pltpu.SemaphoreType.DMA((3,))],
         compiler_params=pltpu.CompilerParams(vmem_limit_bytes=VMEM_BYTES),
-    )(*results)
+    )(*parts)
     return smoothed, residual, coarse_rhs.reshape(coarse_source.shape)
 
 

time: 65.9 us -> 36.9 us (0.56)
  Pallas kernels: 65.1 us -> 36.1 us
    pallas_call x1, Pallas kernels: 25 us -> 2.15 us  [per_device(): pl.pallas_call(hand_out_kernel, out_shape=tuple((jax.ShapeDtypeStruct(par...]
    pallas_call x1, Pallas kernels: 40.2 us -> 33.9 us  [per_device(): pl.pallas_call(functools.partial(level_kernel, coarse_slots), out_shape=(...]
where the time goes in v3:
time: 36.9 us; the launch traced here: 36.7 us
  Pallas kernels  36.1 us (98%)
  between operations  0.64 us (2%)
    pallas_call x1, Pallas kernels, per_device(): pl.pallas_call(functools.partial(level_kernel, coarse_slots), out_shape=(...  33.9 us
    pallas_call x1, Pallas kernels, per_device(): pl.pallas_call(hand_out_kernel, out_shape=tuple((jax.ShapeDtypeStruct(par...  2.15 us

profile of v3, /device:TPU:0, one launch (start us, length us, event | category | flops | bytes accessed | tf_op | source)
XLA Modules:
  0.0 36.7 jit_solution(7412631510253466954)
XLA Ops:
  0.6 33.9 %shard_map.76 = (f32[1,2,32,1024]{3,2,1,0:T(8,128)}, f32[1,2,32,1024]{3,2,1,0:T(8,128)}, f32[4,2,24,256]{3,2,1,0:T(8,128)}) custom-call(f32[3,1,4,32,1024]{4,3,2,1,0:T(8,128)} %old_ref.1, s32[1,8]{1,0:T(1,128)} %count_hbm.1, s32[1,2,6]{2,1,0:T(2,128)} %link_hbm.1, s32[1,2,3]{2,1,0:T(2,128)} %parent_hbm.1), custom_call_target="tpu_custom_call" | custom-call | tf_op jit(solution)/shard_map/pallas_call | solution.py:631
  34.6 2.1 %shard_map.77 = (f32[1,2,32,1024]{3,2,1,0:T(8,128)}, f32[1,2,32,1024]{3,2,1,0:T(8,128)}, f32[16,16,256]{2,1,0:T(8,128)}) custom-call(f32[1,2,32,1024]{3,2,1,0:T(8,128)} %get-tuple-element.9.smooth_in, f32[1,2,32,1024]{3,2,1,0:T(8,128)} %get-tuple-element.10.residual_in, f32[4,2,24,256]{3,2,1,0:T(8,128)} %get-tuple-element.11.packs_in, f32[16,16,256]{2,1,0:T(8,128)} %bitcast.2), custom_call_target="tpu_custom_call" | custom-call | tf_op jit(solution)/shard_map/pallas_call | solution.py:653

commit v4 on v3

--- a/solution.py
+++ b/solution.py
@@ -202,11 +202,11 @@
                 half_out[part - 1, side, :, rows, :] = thin(
                     spread(held[field][slot, rows, :]), colour
                 )
-        move_start(part)
 
     move_start(0)
     load(0).wait()
     thin_out(1, 0, 1)
+    move_start(1)
     load(1).wait()
     thin_out(2, 1, 0)
     thin_out(3, 1, 1)
@@ -346,6 +346,7 @@
                 2, b, t, lambda side, rows: spread(coef_in[side, rows, :])
             )
     faces_start(0, own_planes(coef))
+    move_start(2)
     move_wait(1)
     for b in range(boxes):
         for t in range(tiles):
@@ -353,6 +354,7 @@
                 0, b, t, lambda side, rows: thicken(half_in[0, side, :, rows, :])
             )
     faces_start(1, own_planes(sol))
+    move_start(3)
     faces_wait(0)
     ghost_rows(0, coef, True)
     for b in range(boxes):

time: 36.9 us -> 35.9 us (0.973)
  Pallas kernels: 36.1 us -> 35 us
    pallas_call x1, Pallas kernels: 33.9 us -> 32.8 us  [per_device(): pl.pallas_call(functools.partial(level_kernel, coarse_slots), out_shape=(...]
where the time goes in v4:
time: 35.9 us; the launch traced here: 35.6 us
  Pallas kernels  35 us (97%)
  between operations  0.64 us (2%)
    pallas_call x1, Pallas kernels, per_device(): pl.pallas_call(functools.partial(level_kernel, coarse_slots), out_shape=(...  32.8 us
    pallas_call x1, Pallas kernels, per_device(): pl.pallas_call(hand_out_kernel, out_shape=tuple((jax.ShapeDtypeStruct(par...  2.15 us

profile of v4, /device:TPU:0, one launch (start us, length us, event | category | flops | bytes accessed | tf_op | source)
XLA Modules:
  0.0 35.6 jit_solution(10896033704321962749)
XLA Ops:
  0.6 32.8 %shard_map.76 = (f32[1,2,32,1024]{3,2,1,0:T(8,128)}, f32[1,2,32,1024]{3,2,1,0:T(8,128)}, f32[4,2,24,256]{3,2,1,0:T(8,128)}) custom-call(f32[3,1,4,32,1024]{4,3,2,1,0:T(8,128)} %old_ref.1, s32[1,8]{1,0:T(1,128)} %count_hbm.1, s32[1,2,6]{2,1,0:T(2,128)} %link_hbm.1, s32[1,2,3]{2,1,0:T(2,128)} %parent_hbm.1), custom_call_target="tpu_custom_call" | custom-call | tf_op jit(solution)/shard_map/pallas_call | solution.py:633
  33.4 2.1 %shard_map.77 = (f32[1,2,32,1024]{3,2,1,0:T(8,128)}, f32[1,2,32,1024]{3,2,1,0:T(8,128)}, f32[16,16,256]{2,1,0:T(8,128)}) custom-call(f32[1,2,32,1024]{3,2,1,0:T(8,128)} %get-tuple-element.9.smooth_in, f32[1,2,32,1024]{3,2,1,0:T(8,128)} %get-tuple-element.10.residual_in, f32[4,2,24,256]{3,2,1,0:T(8,128)} %get-tuple-element.11.packs_in, f32[16,16,256]{2,1,0:T(8,128)} %bitcast.2), custom_call_target="tpu_custom_call" | custom-call | tf_op jit(solution)/shard_map/pallas_call | solution.py:655

commit v5 on v4

--- a/solution.py
+++ b/solution.py
@@ -35,6 +35,8 @@
     coef_in,
     half_out,
     half_in,
+    rows_out,
+    rows_in,
     sol,
     coef,
     weights,
@@ -175,8 +177,10 @@
     def move(side, part):
         if part == 0:
             source, target = coef_out.at[side], coef_in.at[side]
+        elif part == 1:
+            source, target = half_out.at[side], half_in.at[side]
         else:
-            source, target = half_out.at[part - 1, side], half_in.at[part - 1, side]
+            source, target = rows_out.at[part - 2, side], rows_in.at[part - 2, side]
         return pltpu.make_async_remote_copy(
             src_ref=source,
             dst_ref=target,
@@ -195,21 +199,20 @@
         def _():
             move(1, part).start()
 
-    def thin_out(part, field, colour):
-        for side, slot in ((0, 0), (1, right_slot)):
-            for t in range(tiles):
-                rows = slice(t * TILE, (t + 1) * TILE)
-                half_out[part - 1, side, :, rows, :] = thin(
-                    spread(held[field][slot, rows, :]), colour
-                )
-
+    outer = [0, tiles - 1]
+    inner = list(range(1, tiles - 1))
     move_start(0)
     load(0).wait()
-    thin_out(1, 0, 1)
+    for side, slot in ((0, 0), (1, right_slot)):
+        for t in range(tiles):
+            rows = slice(t * TILE, (t + 1) * TILE)
+            half_out[side, :, rows, :] = thin(spread(held_sol[slot, rows, :]), 1)
     move_start(1)
     load(1).wait()
-    thin_out(2, 1, 0)
-    thin_out(3, 1, 1)
+    for side, slot in ((0, 0), (1, right_slot)):
+        for part, which in ((0, outer), (1, inner)):
+            for i, t in enumerate(which):
+                rows_out[part, side, i] = held_rhs[slot, t * TILE : (t + 1) * TILE, :]
 
     def move_wait(part):
         @pl.when(has_right)
@@ -351,7 +354,7 @@
     for b in range(boxes):
         for t in range(tiles):
             sol[b, :, PAD + t * TILE : PAD + (t + 1) * TILE, :] = moved(
-                0, b, t, lambda side, rows: thicken(half_in[0, side, :, rows, :])
+                0, b, t, lambda side, rows: thicken(half_in[side, :, rows, :])
             )
     faces_start(1, own_planes(sol))
     move_start(3)
@@ -387,11 +390,13 @@
         ],
     )
 
-    def scale_rhs(part, arrived):
+    def scale_rhs(part, which):
         move_wait(part)
         for b in range(boxes):
-            for t in range(tiles):
-                scaled_rhs[b, t] = inverse[b, t] * moved(1, b, t, arrived)
+            for i, t in enumerate(which):
+                scaled_rhs[b, t] = inverse[b, t] * moved(
+                    1, b, t, lambda side, rows, i=i: spread(rows_in[part - 2, side, i])
+                )
 
     def relaxed(b, t):
         here, near = around(sol, b, t)
@@ -399,9 +404,6 @@
         for f in range(FACES):
             total = total + weights[b, t, f] * near[f]
         return here, total
-
-    inner = list(range(1, tiles - 1))
-    outer = [0, tiles - 1] if tiles > 1 else [0]
 
     def sweep(colour, which):
         for b in range(boxes):
@@ -411,7 +413,6 @@
                     parity == colour, total, here
                 )
 
-    scale_rhs(2, lambda side, rows: thicken(half_in[1, side, :, rows, :]))
     def next_planes(colour):
         def plane_of(b, side):
             t = side * (tiles - 1)
@@ -425,19 +426,13 @@
 
         return plane_of
 
-    sweep(0, inner)
     faces_wait(1)
     ghost_rows(1, sol, False)
+    scale_rhs(2, outer)
     sweep(0, outer)
-    scale_rhs(
-        3,
-        lambda side, rows: jnp.where(
-            parity == 0,
-            thicken(half_in[1, side, :, rows, :]),
-            thicken(half_in[2, side, :, rows, :]),
-        ),
-    )
     faces_start(3, next_planes(1))
+    scale_rhs(3, inner)
+    sweep(0, inner)
     sweep(1, inner)
     faces_wait(2)
     faces_wait(3)
@@ -453,14 +448,6 @@
     sweep(1, outer)
     advance_ghosts(1)
 
-    for b in range(boxes):
-        for t in range(tiles):
-            plane_out[b, t * TILE : (t + 1) * TILE, :] = flatten(
-                sol[b, :, PAD + t * TILE : PAD + (t + 1) * TILE, :]
-            )
-    smooth_store = pltpu.make_async_copy(plane_out, smooth_out.at[0], store_sem.at[0])
-    smooth_store.start()
-
     def leave(which):
         for b in range(boxes):
             for t in which:
@@ -504,6 +491,13 @@
 
     for step in range(1, groups):
         pack_to(step).start()
+    for b in range(boxes):
+        for t in range(tiles):
+            plane_out[b, t * TILE : (t + 1) * TILE, :] = flatten(
+                sol[b, :, PAD + t * TILE : PAD + (t + 1) * TILE, :]
+            )
+    smooth_store = pltpu.make_async_copy(plane_out, smooth_out.at[0], store_sem.at[0])
+    smooth_store.start()
     own_store = pltpu.make_async_copy(pack, packs_out.at[0], store_sem.at[2])
     own_store.start()
     for step in range(1, groups):
@@ -604,8 +598,10 @@
         pltpu.VMEM((slots, edge, cells), f32),
         pltpu.VMEM((2, edge, cells), f32),
         pltpu.VMEM((2, edge, cells), f32),
-        pltpu.VMEM((3, 2, columns // 2, edge, LANES), f32),
-        pltpu.VMEM((3, 2, columns // 2, edge, LANES), f32),
+        pltpu.VMEM((2, columns // 2, edge, LANES), f32),
+        pltpu.VMEM((2, columns // 2, edge, LANES), f32),
+        pltpu.VMEM((2, 2, tiles // 2, TILE, cells), f32),
+        pltpu.VMEM((2, 2, tiles // 2, TILE, cells), f32),
         pltpu.VMEM((boxes, columns, padded, LANES), f32),
         pltpu.VMEM((boxes, columns, padded, LANES), f32),
         pltpu.VMEM((boxes, tiles, FACES, columns, TILE, LANES), f32),

time: 35.9 us -> 35.1 us (0.978)
  the two profiles are of different devices: /device:TPU:0 before, /device:TPU:3 now
where the time goes in v5:
time: 35.1 us; the launch traced here: 34.9 us
  Pallas kernels  34.3 us (98%)
  between operations  0.64 us (2%)
    pallas_call x1, Pallas kernels, per_device(): pl.pallas_call(functools.partial(level_kernel, coarse_slots), out_shape=(...  32.1 us
    pallas_call x1, Pallas kernels, per_device(): pl.pallas_call(hand_out_kernel, out_shape=tuple((jax.ShapeDtypeStruct(par...  2.15 us

profile of v5, /device:TPU:3, one launch (start us, length us, event | category | flops | bytes accessed | tf_op | source)
XLA Modules:
  0.0 34.9 jit_solution(10922206408766308586)
XLA Ops:
  0.6 32.1 %shard_map.76 = (f32[1,2,32,1024]{3,2,1,0:T(8,128)}, f32[1,2,32,1024]{3,2,1,0:T(8,128)}, f32[4,2,24,256]{3,2,1,0:T(8,128)}) custom-call(f32[3,1,4,32,1024]{4,3,2,1,0:T(8,128)} %old_ref.1, s32[1,8]{1,0:T(1,128)} %count_hbm.1, s32[1,2,6]{2,1,0:T(2,128)} %link_hbm.1, s32[1,2,3]{2,1,0:T(2,128)} %parent_hbm.1), custom_call_target="tpu_custom_call" | custom-call | tf_op jit(solution)/shard_map/pallas_call | solution.py:629
  32.8 2.1 %shard_map.77 = (f32[1,2,32,1024]{3,2,1,0:T(8,128)}, f32[1,2,32,1024]{3,2,1,0:T(8,128)}, f32[16,16,256]{2,1,0:T(8,128)}) custom-call(f32[1,2,32,1024]{3,2,1,0:T(8,128)} %get-tuple-element.9.smooth_in, f32[1,2,32,1024]{3,2,1,0:T(8,128)} %get-tuple-element.10.residual_in, f32[4,2,24,256]{3,2,1,0:T(8,128)} %get-tuple-element.11.packs_in, f32[16,16,256]{2,1,0:T(8,128)} %bitcast.2), custom_call_target="tpu_custom_call" | custom-call | tf_op jit(solution)/shard_map/pallas_call | solution.py:651

commit v6 on v5

--- a/solution.py
+++ b/solution.py
@@ -213,6 +213,7 @@
         for part, which in ((0, outer), (1, inner)):
             for i, t in enumerate(which):
                 rows_out[part, side, i] = held_rhs[slot, t * TILE : (t + 1) * TILE, :]
+    move_start(2)
 
     def move_wait(part):
         @pl.when(has_right)
@@ -349,7 +350,6 @@
                 2, b, t, lambda side, rows: spread(coef_in[side, rows, :])
             )
     faces_start(0, own_planes(coef))
-    move_start(2)
     move_wait(1)
     for b in range(boxes):
         for t in range(tiles):
@@ -562,10 +562,8 @@
     ]
     for load in loads:
         load.start()
-    for load in loads:
-        load.wait()
-    stores[0].start()
-    stores[1].start()
+    loads[0].wait()
+    loads[1].wait()
     for source in range(groups):
         for b in range(boxes):
             label = packs[source, b, half : half + TILE, :]
@@ -575,6 +573,9 @@
                 mine = (group * slots + s).astype(jnp.float32)
                 coarse[s] = jnp.where(label == mine, values, coarse[s])
     stores[2].start()
+    for i in range(2):
+        loads[2 + i].wait()
+        stores[i].start()
     for store in stores:
         store.wait()
 

time: 35.1 us -> 34.3 us (0.977)
  the two profiles are of different devices: /device:TPU:3 before, /device:TPU:0 now
where the time goes in v6:
time: 34.3 us; the launch traced here: 34.1 us
  Pallas kernels  33.5 us (98%)
  between operations  0.64 us (2%)
    pallas_call x1, Pallas kernels, per_device(): pl.pallas_call(functools.partial(level_kernel, coarse_slots), out_shape=(...  31.3 us
    pallas_call x1, Pallas kernels, per_device(): pl.pallas_call(hand_out_kernel, out_shape=tuple((jax.ShapeDtypeStruct(par...  2.15 us

profile of v6, /device:TPU:0, one launch (start us, length us, event | category | flops | bytes accessed | tf_op | source)
XLA Modules:
  0.0 34.1 jit_solution(11863613912842367079)
XLA Ops:
  0.6 31.3 %shard_map.76 = (f32[1,2,32,1024]{3,2,1,0:T(8,128)}, f32[1,2,32,1024]{3,2,1,0:T(8,128)}, f32[4,2,24,256]{3,2,1,0:T(8,128)}) custom-call(f32[3,1,4,32,1024]{4,3,2,1,0:T(8,128)} %old_ref.1, s32[1,8]{1,0:T(1,128)} %count_hbm.1, s32[1,2,6]{2,1,0:T(2,128)} %link_hbm.1, s32[1,2,3]{2,1,0:T(2,128)} %parent_hbm.1), custom_call_target="tpu_custom_call" | custom-call | tf_op jit(solution)/shard_map/pallas_call | solution.py:630
  32.0 2.1 %shard_map.77 = (f32[1,2,32,1024]{3,2,1,0:T(8,128)}, f32[1,2,32,1024]{3,2,1,0:T(8,128)}, f32[16,16,256]{2,1,0:T(8,128)}) custom-call(f32[1,2,32,1024]{3,2,1,0:T(8,128)} %get-tuple-element.9.smooth_in, f32[1,2,32,1024]{3,2,1,0:T(8,128)} %get-tuple-element.10.residual_in, f32[4,2,24,256]{3,2,1,0:T(8,128)} %get-tuple-element.11.packs_in, f32[16,16,256]{2,1,0:T(8,128)} %bitcast.2), custom_call_target="tpu_custom_call" | custom-call | tf_op jit(solution)/shard_map/pallas_call | solution.py:652

commit v7 on v6

--- a/solution.py
+++ b/solution.py
@@ -350,6 +350,7 @@
                 2, b, t, lambda side, rows: spread(coef_in[side, rows, :])
             )
     faces_start(0, own_planes(coef))
+    move_start(3)
     move_wait(1)
     for b in range(boxes):
         for t in range(tiles):
@@ -357,7 +358,6 @@
                 0, b, t, lambda side, rows: thicken(half_in[side, :, rows, :])
             )
     faces_start(1, own_planes(sol))
-    move_start(3)
     faces_wait(0)
     ghost_rows(0, coef, True)
     for b in range(boxes):

time: 34.3 us -> 35.9 us (1.047)
  Pallas kernels: 33.5 us -> 35.1 us
    pallas_call x1, Pallas kernels: 31.3 us -> 33 us  [per_device(): pl.pallas_call(functools.partial(level_kernel, coarse_slots), out_shape=(...]
where the time goes in v7:
time: 35.9 us; the launch traced here: 35.8 us
  Pallas kernels  35.1 us (98%)
  between operations  0.64 us (2%)
    pallas_call x1, Pallas kernels, per_device(): pl.pallas_call(functools.partial(level_kernel, coarse_slots), out_shape=(...  33 us
    pallas_call x1, Pallas kernels, per_device(): pl.pallas_call(hand_out_kernel, out_shape=tuple((jax.ShapeDtypeStruct(par...  2.15 us

profile of v7, /device:TPU:0, one launch (start us, length us, event | category | flops | bytes accessed | tf_op | source)
XLA Modules:
  0.0 35.8 jit_solution(17132527482732929513)
XLA Ops:
  0.6 33.0 %shard_map.76 = (f32[1,2,32,1024]{3,2,1,0:T(8,128)}, f32[1,2,32,1024]{3,2,1,0:T(8,128)}, f32[4,2,24,256]{3,2,1,0:T(8,128)}) custom-call(f32[3,1,4,32,1024]{4,3,2,1,0:T(8,128)} %old_ref.1, s32[1,8]{1,0:T(1,128)} %count_hbm.1, s32[1,2,6]{2,1,0:T(2,128)} %link_hbm.1, s32[1,2,3]{2,1,0:T(2,128)} %parent_hbm.1), custom_call_target="tpu_custom_call" | custom-call | tf_op jit(solution)/shard_map/pallas_call | solution.py:630
  33.6 2.1 %shard_map.77 = (f32[1,2,32,1024]{3,2,1,0:T(8,128)}, f32[1,2,32,1024]{3,2,1,0:T(8,128)}, f32[16,16,256]{2,1,0:T(8,128)}) custom-call(f32[1,2,32,1024]{3,2,1,0:T(8,128)} %get-tuple-element.9.smooth_in, f32[1,2,32,1024]{3,2,1,0:T(8,128)} %get-tuple-element.10.residual_in, f32[4,2,24,256]{3,2,1,0:T(8,128)} %get-tuple-element.11.packs_in, f32[16,16,256]{2,1,0:T(8,128)} %bitcast.2), custom_call_target="tpu_custom_call" | custom-call | tf_op jit(solution)/shard_map/pallas_call | solution.py:652
